TPU v7x, 512 devices: a whole 4x8x8 slice. The times are simulated.
512 devices in a mesh: gx: 16 (over y, core), yz: 32 (over x, z).
Axes of the slice: x: 4, y: 8, z: 8, core: 2. Of those that a mesh axis runs over, the one named last changes fastest.
Arguments:
- stiffness: bfloat16 [16, 32, 8, 27, 9216], P('gx', 'yz'), may hold values from -0.625 to 0.625
- prolong: bfloat16 [16, 32, 8, 96, 128], P('gx', 'yz'), may hold values from -1.5 to 1.5
- kcol: int32 [16, 32, 8, 27], P('gx', 'yz'), may hold values from 0 to 15
- kcount: int32 [16, 32, 8], P('gx', 'yz'), may hold values from 24 to 27
- qslot: int32 [16, 32, 8, 27, 2], P('gx', 'yz'), may hold values from 0 to 2
- glist: int32 [16, 32, 4, 2], P('gx', 'yz'), may hold values from 0 to 7
- owner: int32 [16, 32, 16, 1], P('gx', 'yz'), may hold values from 0 to 31; in each aligned block of 16 rows (0 to 15, 16 to 31, ..., all dimensions but the last counted through in order) at most 2 rows name the same one
- dest: int32 [16, 32, 16, 3], P('gx', 'yz'), may hold values from 0 to 47
Outputs:
- coarse: float32 [16, 32, 48, 4096], P('gx', 'yz')
Inputs may be any that keep to these rules, and one draw needn't show every extreme that they name: Among the 16 pairs of one device no owner occurs more than 2 times; some device has an owner exactly 2 times, and every owner occurs somewhere.
All inputs are finite; a program needn't handle non-finite values.
Results may differ from a plain program's by a relative error of at most 0.0029.
Values may be sent and summed in bfloat16 or wider, within the bound.
No kernel may reach another device: no remote copies, remote signals or barrier semaphores. Data moves between devices by JAX's collectives and lax.ppermute only.
A program may use at most 128 MiB of HBM per device.

v0:
```python
import jax
import jax.numpy as jnp
from jax import lax
from jax.sharding import PartitionSpec as P

BP = 64
PW = 2
QW = 3
NS = 48


def padded(shard, sides, width):
    for axis, dim in sides:
        size, length = (lax.axis_size(axis), shard.shape[dim])
        up = [(i, (i + 1) % size) for i in range(size - 1)]
        down = [(j, i) for i, j in up]
        last = lax.slice_in_dim(shard, length - width, length, axis=dim)
        first = lax.slice_in_dim(shard, 0, width, axis=dim)
        before = lax.ppermute(last, axis, up)
        after = lax.ppermute(first, axis, down)
        shard = jnp.concatenate([before, shard, after], axis=dim)
    return shard


def on_device(stiffness, prolong, kcol, kcount, qslot, glist, owner, dest):
    blocks_flat = stiffness[0, 0]
    prolong_rows = prolong[0, 0]
    row_count, block_width, packed_width = prolong_rows.shape
    slot_count = blocks_flat.shape[1]
    ghost_lists = glist[0, 0]
    ghost_depth = ghost_lists.shape[1]
    picked = prolong_rows[ghost_lists]
    slab_send = jnp.concatenate([picked[0], picked[1]], 0)
    slab_ext = padded(slab_send, (("gx", 0),), ghost_depth)
    column_send = jnp.concatenate([picked[2], picked[3]], 0)
    column_ext = padded(column_send, (("yz", 0),), ghost_depth)
    extended = jnp.concatenate(
        [
            prolong_rows,
            slab_ext[:ghost_depth],
            slab_ext[3 * ghost_depth :],
            column_ext[:ghost_depth],
            column_ext[3 * ghost_depth :],
        ],
        0,
    )
    gathered = extended[kcol[0, 0]]
    square = blocks_flat.reshape(row_count, slot_count, block_width, block_width)
    product = jnp.einsum("itab,itbc->itac", square, gathered, preferred_element_type=jnp.float32)
    live_slot = (jnp.arange(slot_count)[None, :] < kcount[0, 0][:, None]).astype(jnp.float32)
    choose = (qslot[0, 0][..., None] == jnp.arange(QW)[None, None, None, :]).astype(jnp.float32)
    choose = choose * live_slot[:, :, None, None]
    split_terms = product.reshape(row_count, slot_count, block_width, PW, BP)
    merged = jnp.einsum(
        "itksc,itsq->ikqc", split_terms, choose, precision=lax.Precision.HIGHEST
    ).astype(jnp.bfloat16)
    pair_prolong = jnp.transpose(prolong_rows.reshape(row_count, block_width, PW, BP), (0, 2, 1, 3))
    pair_prolong = pair_prolong.reshape(row_count * PW, block_width, BP)
    pair_merged = jnp.repeat(merged, PW, axis=0)
    owners = owner[0, 0, :, 0]
    targets = dest[0, 0]
    pair_count = owners.shape[0]
    peer_count = lax.axis_size("yz")
    capacity = max(2, (3 * pair_count + peer_count - 1) // peer_count)
    owner_marks = (owners[:, None] == jnp.arange(peer_count)[None, :]).astype(jnp.int32)
    before = jnp.cumsum(owner_marks, 0) - owner_marks
    position = jnp.sum(before * owner_marks, 1)
    place_index = owners * capacity + position
    source = (
        jnp.full((peer_count * capacity,), -1, jnp.int32)
        .at[place_index]
        .set(jnp.arange(pair_count, dtype=jnp.int32))
    )
    filled = source >= 0
    chosen = jnp.maximum(source, 0)
    slot_targets = jnp.where(filled[:, None], targets[chosen], NS).reshape(peer_count, capacity, QW)
    payload = jnp.concatenate([pair_prolong[:, :, None, :], pair_merged], 2)
    payload = payload.reshape(pair_count, block_width, (QW + 1) * BP)
    packed_rows = payload[chosen].reshape(peer_count, capacity, block_width, (QW + 1) * BP)
    arrived = lax.all_to_all(packed_rows, "yz", split_axis=0, concat_axis=0, tiled=True)
    labels_in = lax.all_to_all(slot_targets, "yz", split_axis=0, concat_axis=0, tiled=True)
    shaped = arrived.reshape(arrived.shape[0], arrived.shape[1], block_width, QW + 1, BP)
    products_here = jnp.einsum(
        "yrkp,yrkqc->yrqpc",
        shaped[:, :, :, 0, :],
        shaped[:, :, :, 1:, :],
        preferred_element_type=jnp.float32,
    )
    products_here = products_here.reshape(arrived.shape[0], arrived.shape[1], QW, BP * BP)
    coarse = jax.ops.segment_sum(
        products_here.reshape(-1, BP * BP), labels_in.reshape(-1), num_segments=NS + 1
    )[:NS]
    return coarse[None, None]


def solution(mesh):
    in_specs = (
        P("gx", "yz", None, None, None),
        P("gx", "yz", None, None, None),
        P("gx", "yz", None, None),
        P("gx", "yz", None),
        P("gx", "yz", None, None, None),
        P("gx", "yz", None, None),
        P("gx", "yz", None, None),
        P("gx", "yz", None, None),
    )
    out_specs = P("gx", "yz", None, None)
    return jax.shard_map(
        on_device, mesh=mesh, in_specs=in_specs, out_specs=out_specs, check_vma=False
    )
```

profile of v0, /device:TPU:24, one launch (start us, length us, event | category | flops | bytes accessed | tf_op | source)
XLA Modules:
  0.0 216.1 jit_solution(15468337595381305184)
XLA Ops:
  0.0 0.7 fusion.23
  0.8 0.8 select_reduce_fusion
  1.6 0.7 fusion.25
  2.3 0.6 scatter_custom_fusion
  2.9 0.7 compare_select_fusion.1
  3.8 1.5 gather_fusion.1
  5.3 1.9 collective-permute-start
  7.3 3.6 %collective-permute-start.1 = (bf16[2,96,128]{2,1,0:T(8,128)(2,1)S(1)}, bf16[2,96,128]{2,1,0:T(8,128)(2,1)S(1)}, u32[]{:S(2)}, u32[]{:S(2)}) collective-permute-start(bf16[2,96,128]{2,1,0:T(8,128)(2,1)S(1)} %get-tuple-element.7), channel_id=1, source_target_pairs={{32,0},{64,32},{96,64},{128,96},{160,128},{192,160},{224,192},{256... | collective-permute-start | bytes 147464 | tf_op jit(solution)/shard_map/ppermute | solution.py:20
  10.9 4.3 %collective-permute-start.2 = (bf16[2,96,128]{2,1,0:T(8,128)(2,1)S(1)}, bf16[2,96,128]{2,1,0:T(8,128)(2,1)S(1)}, u32[]{:S(2)}, u32[]{:S(2)}) collective-permute-start(bf16[2,96,128]{2,1,0:T(8,128)(2,1)S(1)} %get-tuple-element.6), channel_id=1, source_target_pairs={{0,1},{1,2},{2,3},{3,4},{4,5},{5,6},{6,7},{7,8},{8,9},{9,10},{10,1... | collective-permute-start | bytes 147464 | tf_op jit(solution)/shard_map/ppermute | solution.py:19
  15.2 1.3 collective-permute-start.3
  16.5 0.8 copy.38
  18.0 0.7 broadcast_select_fusion
  18.7 14.6 %all-to-all-start = ((s32[32,2,3]{2,1,0:T(2,128)}), s32[32,2,3]{2,1,0:T(2,128)S(1)}, u32[]{:S(2)}, u32[]{:S(2)}) async-start(s32[32,2,3]{2,1,0:T(2,128)} %broadcast_select_fusion), calls=%async_computation | async-start | bytes 65536 | tf_op jit(solution)/shard_map/all_to_all | solution.py:81
  33.3 0.9 constant_dynamic-update-slice_fusion.4
  34.3 0.7 compare_select_fusion
  35.0 0.7 fusion.24
  35.8 1.1 copy.25
  36.9 8.9 %reshape_squeeze.7 = bf16[8,27,96,96]{3,2,0,1:T(8,128)(2,1)} reshape(bf16[1,1,8,27,9216]{4,2,3,1,0:T(8,128)(2,1)} %param.8) | data formatting | bytes 7962624 | tf_op jit(solution)/shard_map/reshape;squeeze | solution.py:48
  45.9 3.6 %gather_fusion.2 = bf16[216,96,128]{2,1,0:T(8,128)(2,1)} fusion(bf16[16,96,128]{2,1,0:T(8,128)(2,1)S(1)} %constant_dynamic-update-slice_fusion, s32[1024]{0:T(1024)S(1)} %pad_clamp_fusion), kind=kCustom, calls=%fused_computation.2 | custom fusion | bytes 10617696 | tf_op jit(solution)/shard_map/gather | solution.py:47
  49.6 9.5 %fusion.4 = f32[8,27,96,128]{3,2,1,0:T(8,128)} fusion(bf16[8,27,96,128]{3,2,1,0:T(8,128)(2,1)} %bitcast.71, bf16[8,27,96,96]{3,2,0,1:T(8,128)(2,1)} %reshape_squeeze.7), kind=kOutput, calls=%fused_computation.10 | convolution fusion | flops 509607936 | bytes 19906560 | tf_op jit(solution)/shard_map/itab,itbc->itac/dot_general | solution.py:49
  59.0 12.5 %copy.28 = f32[8,27,96,128]{2,3,1,0:T(8,128)} copy(f32[8,27,96,128]{3,2,1,0:T(8,128)} %fusion.4) | data formatting | bytes 21233664 | tf_op jit(solution)/shard_map/itab,itbc->itac/dot_general | solution.py:49
  71.5 20.7 %fusion.13 = bf16[8,96,3,64]{1,2,3,0:T(4,128)(2,1)S(1)} fusion(f32[8,27,96,2,64]{2,4,3,1,0:T(8,128)} %bitcast.70, f32[8,27]{1,0:T(8,128)S(1)} %fusion.24, s32[8,27,2]{1,2,0:T(2,128)S(1)} %bitcast.80), kind=kOutput, calls=%fused_computation.14 | convolution fusion | flops 95701536 | bytes 10914336 | tf_op jit(solution)/shard_map/itksc,itsq->ikqc/dot_general | solution.py:54
  92.8 3.0 %gather_fusion.3 = bf16[64,96,256]{1,2,0:T(8,128)(2,1)} fusion(bf16[16,96,256]{1,2,0:T(8,128)(2,1)S(1)} %bitcast.73, s32[1024]{0:T(1024)S(1)} %get-tuple-element.10), kind=kCustom, calls=%fused_computation.3 | custom fusion | bytes 6291712 | tf_op jit(solution)/shard_map/gather | solution.py:79
  95.8 6.2 %copy.31 = bf16[32,2,96,256]{3,2,1,0:T(8,128)(2,1)} copy(bf16[32,2,96,256]{2,3,1,0:T(8,128)(2,1)} %bitcast.74) | data formatting | bytes 6291456 | tf_op jit(solution)/shard_map/reshape | solution.py:79
  102.0 10.0 %all-to-all-start.1 = ((bf16[32,2,96,256]{3,2,1,0:T(8,128)(2,1)}), bf16[32,2,96,256]{3,2,1,0:T(8,128)(2,1)S(1)}, u32[]{:S(2)}, u32[]{:S(2)}) async-start(bf16[32,2,96,256]{3,2,1,0:T(8,128)(2,1)} %copy.31), calls=%async_computation.1 | async-start | bytes 6291456 | tf_op jit(solution)/shard_map/all_to_all | solution.py:80
  112.1 74.7 %all-to-all-done.1 = bf16[32,2,96,256]{3,2,1,0:T(8,128)(2,1)S(1)} async-done(((bf16[32,2,96,256]{3,2,1,0:T(8,128)(2,1)}), bf16[32,2,96,256]{3,2,1,0:T(8,128)(2,1)S(1)}, u32[]{:S(2)}, u32[]{:S(2)}) %all-to-all-start.1) | async-done | bytes 3145760 | tf_op jit(solution)/shard_map/all_to_all | solution.py:80
  186.8 4.0 %copy.32 = bf16[32,2,96,256]{2,3,1,0:T(8,128)(2,1)} copy(bf16[32,2,96,256]{3,2,1,0:T(8,128)(2,1)S(1)} %all-to-all-done.1) | data formatting | bytes 6291456 | tf_op jit(solution)/shard_map/all_to_all | solution.py:80
  190.8 5.8 %convolution_bitcast_fusion = f32[32,2,3,64,64]{3,4,2,1,0:T(8,128)} fusion(bf16[32,2,96,4,64]{2,4,3,1,0:T(8,128)(2,1)} %bitcast.72), kind=kOutput, calls=%fused_computation.11 | convolution fusion | flops 150994944 | bytes 8388608 | tf_op jit(solution)/shard_map/yrkp,yrkqc->yrqpc/dot_general | solution.py:83
  196.7 6.5 %copy.34 = f32[32,2,3,64,64]{4,3,2,1,0:T(8,128)} copy(f32[32,2,3,64,64]{3,4,2,1,0:T(8,128)} %convolution_bitcast_fusion) | data formatting | bytes 6291456 | tf_op jit(solution)/shard_map/yrkp,yrkqc->yrqpc/transpose | solution.py:83
  203.2 5.8 %reshape.183 = f32[192,4096]{1,0:T(8,128)} reshape(f32[32,2,3,64,64]{4,3,2,1,0:T(8,128)} %copy.34) | data formatting | bytes 6291456 | tf_op jit(solution)/shard_map/reshape;reshape | solution.py:91
  209.0 6.1 %scatter_custom_fusion.1 = f32[49,4096]{1,0:T(8,128)S(1)} fusion(s32[192]{0:T(256)S(1)} %reshape.181, f32[192,4096]{1,0:T(8,128)} %reshape.183, f32[]{:T(128)} %constant.8.clone.1), kind=kCustom, calls=%fused_computation.18 | custom fusion | flops 786432 | bytes 803328 | tf_op jit(solution)/shard_map/scatter-add | solution.py:90
  215.2 0.9 slice_bitcast_fusion.2
  (27 shorter events, 1.7 us)
Async XLA Ops:
  5.3 40.5 %collective-permute-start = (bf16[2,96,128]{2,1,0:T(8,128)(2,1)S(1)}, bf16[2,96,128]{2,1,0:T(8,128)(2,1)S(1)}, u32[]{:S(2)}, u32[]{:S(2)}) collective-permute-start(bf16[2,96,128]{2,1,0:T(8,128)(2,1)S(1)} %get-tuple-element.8), channel_id=1, source_target_pairs={{0,32},{32,64},{64,96},{96,128},{128,160},{160,192},{192,224},{224... | collective-permute-start | bytes 147464 | tf_op jit(solution)/shard_map/ppermute | solution.py:19
  7.3 38.6 %collective-permute-start.1 = (bf16[2,96,128]{2,1,0:T(8,128)(2,1)S(1)}, bf16[2,96,128]{2,1,0:T(8,128)(2,1)S(1)}, u32[]{:S(2)}, u32[]{:S(2)}) collective-permute-start(bf16[2,96,128]{2,1,0:T(8,128)(2,1)S(1)} %get-tuple-element.7), channel_id=1, source_target_pairs={{32,0},{64,32},{96,64},{128,96},{160,128},{192,160},{224,192},{256... | collective-permute-start | bytes 147464 | tf_op jit(solution)/shard_map/ppermute | solution.py:20
  10.9 34.9 %collective-permute-start.2 = (bf16[2,96,128]{2,1,0:T(8,128)(2,1)S(1)}, bf16[2,96,128]{2,1,0:T(8,128)(2,1)S(1)}, u32[]{:S(2)}, u32[]{:S(2)}) collective-permute-start(bf16[2,96,128]{2,1,0:T(8,128)(2,1)S(1)} %get-tuple-element.6), channel_id=1, source_target_pairs={{0,1},{1,2},{2,3},{3,4},{4,5},{5,6},{6,7},{7,8},{8,9},{9,10},{10,1... | collective-permute-start | bytes 147464 | tf_op jit(solution)/shard_map/ppermute | solution.py:19
  15.2 30.7 %collective-permute-start.3 = (bf16[2,96,128]{2,1,0:T(8,128)(2,1)S(1)}, bf16[2,96,128]{2,1,0:T(8,128)(2,1)S(1)}, u32[]{:S(2)}, u32[]{:S(2)}) collective-permute-start(bf16[2,96,128]{2,1,0:T(8,128)(2,1)S(1)} %get-tuple-element.5), channel_id=1, source_target_pairs={{1,0},{2,1},{3,2},{4,3},{5,4},{6,5},{7,6},{8,7},{9,8},{10,9},{11,1... | collective-permute-start | bytes 147464 | tf_op jit(solution)/shard_map/ppermute | solution.py:20
  18.7 83.3 %all-to-all-start = ((s32[32,2,3]{2,1,0:T(2,128)}), s32[32,2,3]{2,1,0:T(2,128)S(1)}, u32[]{:S(2)}, u32[]{:S(2)}) async-start(s32[32,2,3]{2,1,0:T(2,128)} %broadcast_select_fusion), calls=%async_computation | async-start | bytes 65536 | tf_op jit(solution)/shard_map/all_to_all | solution.py:81
  59.0 12.5 %copy-start = (s32[1,1,8,27,2]{3,4,2,1,0:T(2,128)S(1)}, s32[1,1,8,27,2]{3,4,2,1,0:T(2,128)}, u32[]{:S(2)}) copy-start(s32[1,1,8,27,2]{3,4,2,1,0:T(2,128)} %param.12) | copy-start | bytes 5188
  102.0 84.9 %all-to-all-start.1 = ((bf16[32,2,96,256]{3,2,1,0:T(8,128)(2,1)}), bf16[32,2,96,256]{3,2,1,0:T(8,128)(2,1)S(1)}, u32[]{:S(2)}, u32[]{:S(2)}) async-start(bf16[32,2,96,256]{3,2,1,0:T(8,128)(2,1)} %copy.31), calls=%async_computation.1 | async-start | bytes 6291456 | tf_op jit(solution)/shard_map/all_to_all | solution.py:80
where the time goes:
time: 217 us; the launch traced here: 216 us
  waiting for transfers between devices  74.8 us (34%)
  local copies, waits for them, and re-layouts  58 us (27%)
  matrix products  36 us (17%)
  starting transfers between devices  35.7 us (16%)
  other arithmetic  11.4 us (5%)
    all_to_all x1, waiting for transfers between devices, on_device(): lax.all_to_all(packed_rows, 'yz', split_axis=0, concat_axis=0, tiled=True)  74.7 us
    dot_general x1, matrix products, on_device(): jnp.einsum('itksc,itsq->ikqc', split_terms, choose, precision=lax.Precisi...  20.7 us
    all_to_all x1, starting transfers between devices, on_device(): lax.all_to_all(slot_targets, 'yz', split_axis=0, concat_axis=0, tiled=True)  14.6 us
    dot_general x1, local copies, waits for them, and re-layouts, on_device(): jnp.einsum('itab,itbc->itac', square, gathered, preferred_element_type=jn...  12.5 us
    all_to_all x1, starting transfers between devices, on_device(): lax.all_to_all(packed_rows, 'yz', split_axis=0, concat_axis=0, tiled=True)  9.96 us
    dot_general x1, matrix products, on_device(): jnp.einsum('itab,itbc->itac', square, gathered, preferred_element_type=jn...  9.49 us
    another operation x1, local copies, waits for them, and re-layouts, on_device(): blocks_flat.reshape(row_count, slot_count, block_width, block_width)  8.93 us
    transpose x1, local copies, waits for them, and re-layouts, on_device(): jnp.einsum('yrkp,yrkqc->yrqpc', shaped[:, :, :, 0, :], shaped[:, :, :, 1:...  6.54 us
  transfers between devices with their start and end apart: 6, of which 1 were waited for; matrix products, arithmetic and copies ran while one was open for 33% of the time, Pallas kernels for 0%

commit v1 on v0

v1 whole, which is shorter than its diff:
```python
import functools
import jax
import jax.numpy as jnp
from jax import lax
from jax.experimental import pallas as pl
from jax.experimental.pallas import tpu as pltpu
from jax.sharding import PartitionSpec as P

BK = 96
BP = 64
KW = 27
PW = 2
QW = 3
NB = 8
G = 2
EXT = NB + 4 * G
M = NB * PW
NS = 48
CAP = 2
LANES = 128
PAIR_ROWS = QW * BP * BP // LANES
SEND_ROWS = CAP * PAIR_ROWS + 8
VMEM_LIMIT = 20 * 1024 * 1024


def pick_kernel(glist_ref, prolong_ref, *out_refs):
    for side, out_ref in enumerate(out_refs):
        for n in range(G):
            out_ref[n] = prolong_ref[glist_ref[n, side]]


def pick_rows(glist, prolong):
    piece = jax.ShapeDtypeStruct((G, BK, PW * BP), jnp.bfloat16)
    return pl.pallas_call(
        pick_kernel,
        out_shape=[piece] * 4,
        in_specs=[pl.BlockSpec(memory_space=pltpu.SMEM), pl.BlockSpec(memory_space=pltpu.VMEM)],
        out_specs=[pl.BlockSpec(memory_space=pltpu.VMEM)] * 4,
        compiler_params=pltpu.CompilerParams(vmem_limit_bytes=VMEM_LIMIT),
        name="pick_rows",
    )(glist, prolong)


def square_kernel(flat_ref, prolong_ref, out_ref, turned_ref, spread_ref):
    lane = lax.broadcasted_iota(jnp.int32, (BK // 4, LANES), 1)
    for t in range(KW):
        for c in range(BK * BK // LANES):
            spread_ref[t % 2, c * NB : (c + 1) * NB, :] = flat_ref[
                t, :, c * LANES : (c + 1) * LANES
            ].astype(jnp.float32)
        for i in range(NB):
            v0, v1, v2 = (
                spread_ref[t % 2, pl.ds(u * NB + i, BK // 4, stride=3 * NB), :] for u in range(3)
            )
            rows = [
                v0,
                pltpu.roll(jnp.where(lane >= 96, v0, v1), 32, 1),
                pltpu.roll(jnp.where(lane >= 64, v1, v2), 64, 1),
                pltpu.roll(v2, 96, 1),
            ]
            out_ref[i, :, t * LANES : (t + 1) * LANES] = jnp.concatenate(rows, 0).astype(
                jnp.bfloat16
            )
    r_from = lax.broadcasted_iota(jnp.int32, (BK, BK), 0)
    r_to = lax.broadcasted_iota(jnp.int32, (BK, BK), 1)
    row_order = (r_from == (r_to % (BK // 4)) * 4 + r_to // (BK // 4)).astype(jnp.bfloat16)
    c_to = lax.broadcasted_iota(jnp.int32, (LANES, LANES), 0)
    c_from = lax.broadcasted_iota(jnp.int32, (LANES, LANES), 1)
    in_pair = c_to % BP
    column_order = (
        c_from == c_to // BP * BP + (in_pair % (BP // 2)) * 2 + in_pair // (BP // 2)
    ).astype(jnp.bfloat16)
    for i in range(NB):
        turned = lax.dot_general(
            column_order, prolong_ref[i], (((1,), (1,)), ((), ())),
            preferred_element_type=jnp.float32,
        ).astype(jnp.bfloat16)
        turned_ref[i] = jnp.dot(
            turned, row_order, preferred_element_type=jnp.float32
        ).astype(jnp.bfloat16)


def square_blocks(flat, prolong):
    vmem = pl.BlockSpec(memory_space=pltpu.VMEM)
    return pl.pallas_call(
        square_kernel,
        out_shape=[
            jax.ShapeDtypeStruct((NB, BK, KW * LANES), jnp.bfloat16),
            jax.ShapeDtypeStruct((NB, LANES, BK), jnp.bfloat16),
        ],
        in_specs=[vmem] * 2,
        out_specs=[vmem] * 2,
        scratch_shapes=[pltpu.VMEM((2, BK * BK // LANES * NB, LANES), jnp.float32)],
        compiler_params=pltpu.CompilerParams(vmem_limit_bytes=VMEM_LIMIT),
        cost_estimate=pl.CostEstimate(flops=0, bytes_accessed=12_000_000, transcendentals=0),
        name="square_blocks",
    )(flat, prolong)


def terms_kernel(
    kcol_ref, kcount_ref, qslot_ref, owner_ref, dest_ref,
    square_ref, turned_ref, prolong_ref, g0_ref, g1_ref, g2_ref, g3_ref,
    send_ref,
    ext_ref, label_ref, count_ref,
):
    peers = send_ref.shape[0]
    lane = lax.broadcasted_iota(jnp.int32, (1, LANES), 1)
    left = lane < BP
    ext_ref[:NB] = prolong_ref[...]
    for n, ghost_ref in enumerate((g0_ref, g1_ref, g2_ref, g3_ref)):
        ext_ref[NB + n * G : NB + (n + 1) * G] = ghost_ref[...]
    label_ref[...] = jnp.full((peers, LANES), float(NS), jnp.float32)
    for o in range(peers):
        count_ref[o] = 0

    def one_row(i, carry):
        live = kcount_ref[i]
        merged = [jnp.zeros((BK, LANES), jnp.float32) for _ in range(QW)]
        for t in range(KW):
            q0 = jnp.where(t < live, qslot_ref[i, 0, t], QW)
            q1 = jnp.where(t < live, qslot_ref[i, 1, t], QW)
            product = jnp.dot(
                square_ref[i, :, t * LANES : t * LANES + BK],
                ext_ref[kcol_ref[i, t]],
                preferred_element_type=jnp.float32,
            )
            column = jnp.where(left, q0, q1)
            for q in range(QW):
                merged[q] += jnp.where(column == q, product, 0.0)
        merged = [part + pltpu.roll(part, BP, 1) for part in merged]
        merged = jnp.concatenate([jnp.where(left, merged[0], merged[1]), merged[2]], 1)
        terms = jnp.dot(
            turned_ref[i], merged.astype(jnp.bfloat16), preferred_element_type=jnp.float32
        )
        for a in range(PW):
            even = terms[a * BP : a * BP + BP // 2]
            odd = terms[a * BP + BP // 2 : (a + 1) * BP]
            even_01, even_2 = even[:, :LANES], even[:, LANES:]
            odd_01, odd_2 = odd[:, :LANES], odd[:, LANES:]
            tiles = [
                jnp.where(left, even_01, pltpu.roll(odd_01, BP, 1)),
                jnp.where(left, pltpu.roll(even_01, BP, 1), odd_01),
                jnp.where(left, even_2, odd_2),
            ]
            m = i * PW + a
            o = owner_ref[m]
            position = count_ref[o]
            count_ref[o] = position + 1
            base = pl.multiple_of(position * PAIR_ROWS, PAIR_ROWS)
            send_ref[o, pl.ds(base, PAIR_ROWS), :] = jnp.concatenate(tiles, 0).astype(jnp.bfloat16)
            label = label_ref[pl.ds(o, 1), :]
            for q in range(QW):
                label = jnp.where(
                    lane == position * QW + q, dest_ref[q, 0, m].astype(jnp.float32), label
                )
            label_ref[pl.ds(o, 1), :] = label
        return carry

    lax.fori_loop(0, NB, one_row, 0)
    for o in range(peers):
        send_ref[o, CAP * PAIR_ROWS :, :] = jnp.broadcast_to(
            label_ref[o : o + 1, :], (8, LANES)
        ).astype(jnp.bfloat16)


def make_terms(kcol, kcount, qslot, owner, dest, squares, turned, prolong, ghosts, peers):
    smem = pl.BlockSpec(memory_space=pltpu.SMEM)
    vmem = pl.BlockSpec(memory_space=pltpu.VMEM)
    return pl.pallas_call(
        terms_kernel,
        out_shape=jax.ShapeDtypeStruct((peers, SEND_ROWS, LANES), jnp.bfloat16),
        in_specs=[smem] * 5 + [vmem] * 7,
        out_specs=vmem,
        scratch_shapes=[
            pltpu.VMEM((EXT, BK, LANES), jnp.bfloat16),
            pltpu.VMEM((peers, LANES), jnp.float32),
            pltpu.SMEM((peers,), jnp.int32),
        ],
        compiler_params=pltpu.CompilerParams(vmem_limit_bytes=VMEM_LIMIT),
        cost_estimate=pl.CostEstimate(
            flops=1_000_000_000, bytes_accessed=8_000_000, transcendentals=0
        ),
        name="make_terms",
    )(kcol, kcount, qslot, owner, dest, squares, turned, prolong, *ghosts)


def sum_kernel(recv_ref, out_ref, acc_ref, label_ref, scalar_ref, sem):
    peers = recv_ref.shape[0]
    for s in range(peers):
        label_ref[s : s + 1, :] = recv_ref[s, CAP * PAIR_ROWS : CAP * PAIR_ROWS + 8, :].astype(
            jnp.float32
        )[:1].astype(jnp.int32)
    copy = pltpu.make_async_copy(label_ref, scalar_ref, sem)
    copy.start()
    rows = BP // 2
    acc_ref[...] = jnp.zeros_like(acc_ref)
    copy.wait()

    def add_source(s, carry):
        for slot in range(CAP):
            @pl.when(scalar_ref[s, slot * QW] < NS)
            def _():
                for q in range(QW):
                    n = scalar_ref[s, slot * QW + q]
                    start = pl.multiple_of(n * rows, rows)
                    base = slot * PAIR_ROWS + q * rows
                    acc_ref[pl.ds(start, rows), :] += recv_ref[s, base : base + rows, :].astype(
                        jnp.float32
                    )

        return carry

    lax.fori_loop(0, peers, add_source, 0)
    for n in range(0, NS, 8):
        for p in range(rows):
            out_ref[n : n + 8, p * LANES : (p + 1) * LANES] = acc_ref[
                pl.ds(n * rows + p, 8, stride=rows), :
            ]


def sum_terms(received):
    return pl.pallas_call(
        sum_kernel,
        out_shape=jax.ShapeDtypeStruct((NS, BP * BP), jnp.float32),
        in_specs=[pl.BlockSpec(memory_space=pltpu.VMEM)],
        out_specs=pl.BlockSpec(memory_space=pltpu.VMEM),
        scratch_shapes=[
            pltpu.VMEM((NS * BP // 2, LANES), jnp.float32),
            pltpu.VMEM((received.shape[0], LANES), jnp.int32),
            pltpu.SMEM((received.shape[0], LANES), jnp.int32),
            pltpu.SemaphoreType.DMA,
        ],
        compiler_params=pltpu.CompilerParams(vmem_limit_bytes=VMEM_LIMIT),
        name="sum_terms",
    )(received)


def on_device(stiffness, prolong, kcol, kcount, qslot, glist, owner, dest):
    prolong_rows = prolong[0, 0]
    picked = pick_rows(jnp.transpose(glist[0, 0]), prolong_rows)
    ghosts = []
    for axis, to_lower, to_upper in (("gx", 0, 1), ("yz", 2, 3)):
        size = lax.axis_size(axis)
        up = [(n, n + 1) for n in range(size - 1)]
        down = [(n + 1, n) for n in range(size - 1)]
        ghosts.append(lax.ppermute(picked[to_upper], axis, up))
        ghosts.append(lax.ppermute(picked[to_lower], axis, down))
    squares, turned = square_blocks(jnp.transpose(stiffness[0, 0], (1, 0, 2)), prolong_rows)
    packed = make_terms(
        kcol[0, 0],
        kcount[0, 0],
        jnp.transpose(qslot[0, 0], (0, 2, 1)),
        owner[0, 0, :, 0],
        jnp.transpose(dest[0, 0])[:, None, :],
        squares, turned, prolong_rows, ghosts, lax.axis_size("yz"),
    )
    received = lax.all_to_all(packed, "yz", split_axis=0, concat_axis=0, tiled=True)
    return sum_terms(received)[None, None]


def solution(mesh):
    split = ("gx", "yz")
    in_specs = tuple(P(*split, *(None,) * n) for n in (3, 3, 2, 1, 3, 2, 2, 2))
    return jax.shard_map(
        on_device, mesh=mesh, in_specs=in_specs, out_specs=P(*split, None, None), check_vma=False
    )
```

time: 217 us -> 85.7 us (0.39)
  waiting for transfers between devices: 74.8 us -> 0.01 us
  blocking collectives: 0 us -> 55.9 us
  local copies, waits for them, and re-layouts: 58 us -> 5.39 us
  matrix products: 36 us -> 0 us
  starting transfers between devices: 35.7 us -> 11.1 us
  Pallas kernels: 0 us -> 12.9 us
  other arithmetic: 11.4 us -> 0 us
    all_to_all x2 -> x0, waiting for transfers between devices: 74.7 us -> none  [the longest x1 74.7 us: on_device(): lax.all_to_all(packed_rows, 'yz', split_axis=0, concat_axis=0, tiled=True)]
    all_to_all x0 -> x1, blocking collectives: none -> 55.9 us  [on_device(): lax.all_to_all(packed, 'yz', split_axis=0, concat_axis=0, tiled=True)]
    dot_general x3 -> x0, matrix products: 36 us -> none  [the longest x1 20.7 us: on_device(): jnp.einsum('itksc,itsq->ikqc', split_terms, choose, precision=lax.Precisi...]
    all_to_all x2 -> x0, starting transfers between devices: 24.6 us -> none  [the longest x1 14.6 us: on_device(): lax.all_to_all(slot_targets, 'yz', split_axis=0, concat_axis=0, tiled=True)]
    another operation x3 -> x0, local copies, waits for them, and re-layouts: 14.9 us -> none  [the longest x1 8.93 us: on_device(): blocks_flat.reshape(row_count, slot_count, block_width, block_width)]
    pallas_call x0 -> x4, Pallas kernels: none -> 12.9 us  [the longest x1 6.89 us: make_terms(): pl.pallas_call(terms_kernel, out_shape=jax.ShapeDtypeStruct((peers, SEND_...]
    dot_general x1 -> x0, local copies, waits for them, and re-layouts: 12.5 us -> none  [on_device(): jnp.einsum('itab,itbc->itac', square, gathered, preferred_element_type=jn...]
    gather x4 -> x0, local copies, waits for them, and re-layouts: 8.79 us -> none  [the longest x1 3.65 us: on_device(): gathered = extended[kcol[0, 0]]]
  transfers between devices with their start and end apart: 6 -> 4, of which waited for: 1 -> 0; matrix products, arithmetic and copies ran while one was open for 33% -> 1% of each run, Pallas kernels for 0% -> 3%
where the time goes in v1:
time: 85.7 us; the launch traced here: 85.4 us
  blocking collectives  55.9 us (65%)
  Pallas kernels  12.9 us (15%)
  starting transfers between devices  11.1 us (13%)
  local copies, waits for them, and re-layouts  5.39 us (6%)
    all_to_all x1, blocking collectives, on_device(): lax.all_to_all(packed, 'yz', split_axis=0, concat_axis=0, tiled=True)  55.9 us
    pallas_call x1, Pallas kernels, make_terms(): pl.pallas_call(terms_kernel, out_shape=jax.ShapeDtypeStruct((peers, SEND_...  6.89 us
    ppermute x2, starting transfers between devices, on_device(): ghosts.append(lax.ppermute(picked[to_upper], axis, up))  6.2 us
    unnamed x17, local copies, waits for them, and re-layouts  5.38 us
    ppermute x2, starting transfers between devices, on_device(): ghosts.append(lax.ppermute(picked[to_lower], axis, down))  4.93 us
    pallas_call x1, Pallas kernels, sum_terms(): pl.pallas_call(sum_kernel, out_shape=jax.ShapeDtypeStruct((NS, BP * BP),...  3.03 us
    pallas_call x1, Pallas kernels, square_blocks(): pl.pallas_call(square_kernel, out_shape=[jax.ShapeDtypeStruct((NB, BK, KW...  2.38 us
  transfers between devices with their start and end apart: 4, of which 0 were waited for; matrix products, arithmetic and copies ran while one was open for 1% of the time, Pallas kernels for 3%

profile of v1, /device:TPU:24, one launch (start us, length us, event | category | flops | bytes accessed | tf_op | source)
XLA Modules:
  0.0 85.4 jit_solution(5879552464460833085)
XLA Ops:
  0.0 0.0 copy-start.7
  0.0 0.0 copy-start.6
  0.0 0.0 copy-start.1
  0.0 0.9 %copy-done.1 = bf16[1,1,8,96,128]{4,3,2,1,0:T(8,128)(2,1)S(1)} copy-done((bf16[1,1,8,96,128]{4,3,2,1,0:T(8,128)(2,1)S(1)}, bf16[1,1,8,96,128]{4,3,2,1,0:T(8,128)(2,1)}, u32[]{:S(2)}) %copy-start.1) | copy-done | bytes 196632
  1.0 0.0 copy-start.5
  1.0 0.7 copy-done.5
  1.6 0.0 copy-start.3
  1.6 0.0 copy-start.4
  1.6 0.6 pick_rows.1
  2.2 1.9 %collective-permute-start = (bf16[2,96,128]{2,1,0:T(8,128)(2,1)S(1)}, bf16[2,96,128]{2,1,0:T(8,128)(2,1)S(1)}, u32[]{:S(2)}, u32[]{:S(2)}) collective-permute-start(bf16[2,96,128]{2,1,0:T(8,128)(2,1)S(1)} %get-tuple-element.13), channel_id=1, source_target_pairs={{0,32},{32,64},{64,96},{96,128},{128,160},{160,192},{192,224},{224... | collective-permute-start | bytes 147464 | tf_op jit(solution)/shard_map/ppermute | solution.py:246
  4.1 3.6 %collective-permute-start.1 = (bf16[2,96,128]{2,1,0:T(8,128)(2,1)S(1)}, bf16[2,96,128]{2,1,0:T(8,128)(2,1)S(1)}, u32[]{:S(2)}, u32[]{:S(2)}) collective-permute-start(bf16[2,96,128]{2,1,0:T(8,128)(2,1)S(1)} %get-tuple-element.14), channel_id=1, source_target_pairs={{32,0},{64,32},{96,64},{128,96},{160,128},{192,160},{224,192},{256... | collective-permute-start | bytes 147464 | tf_op jit(solution)/shard_map/ppermute | solution.py:247
  7.8 4.3 %collective-permute-start.2 = (bf16[2,96,128]{2,1,0:T(8,128)(2,1)S(1)}, bf16[2,96,128]{2,1,0:T(8,128)(2,1)S(1)}, u32[]{:S(2)}, u32[]{:S(2)}) collective-permute-start(bf16[2,96,128]{2,1,0:T(8,128)(2,1)S(1)} %get-tuple-element.15), channel_id=1, source_target_pairs={{0,1},{1,2},{2,3},{3,4},{4,5},{5,6},{6,7},{7,8},{8,9},{9,10},{10,1... | collective-permute-start | bytes 147464 | tf_op jit(solution)/shard_map/ppermute | solution.py:246
  12.1 1.3 %collective-permute-start.3 = (bf16[2,96,128]{2,1,0:T(8,128)(2,1)S(1)}, bf16[2,96,128]{2,1,0:T(8,128)(2,1)S(1)}, u32[]{:S(2)}, u32[]{:S(2)}) collective-permute-start(bf16[2,96,128]{2,1,0:T(8,128)(2,1)S(1)} %get-tuple-element.16), channel_id=1, source_target_pairs={{1,0},{2,1},{3,2},{4,3},{5,4},{6,5},{7,6},{8,7},{9,8},{10,9},{11,1... | collective-permute-start | bytes 147464 | tf_op jit(solution)/shard_map/ppermute | solution.py:247
  13.4 0.7 copy.12
  14.1 0.0 copy-start
  14.1 2.1 %copy-done = bf16[1,1,8,27,9216]{4,2,3,1,0:T(8,128)(2,1)S(1)} copy-done((bf16[1,1,8,27,9216]{4,2,3,1,0:T(8,128)(2,1)S(1)}, bf16[1,1,8,27,9216]{4,2,3,1,0:T(8,128)(2,1)}, u32[]{:S(2)}) %copy-start) | copy-done | bytes 3981336
  16.2 0.0 copy-start.2
  16.2 0.9 %copy-done.2 = bf16[1,1,8,96,128]{4,3,2,1,0:T(8,128)(2,1)S(1)} copy-done((bf16[1,1,8,96,128]{4,3,2,1,0:T(8,128)(2,1)S(1)}, bf16[1,1,8,96,128]{4,3,2,1,0:T(8,128)(2,1)}, u32[]{:S(2)}) %copy-start.2) | copy-done | bytes 196632
  17.1 2.4 %square_blocks.1 = (bf16[8,96,3456]{2,1,0:T(8,128)(2,1)S(1)}, bf16[8,128,96]{2,1,0:T(8,128)(2,1)S(1)}) custom-call(bf16[27,8,9216]{2,1,0:T(8,128)(2,1)S(1)} %bitcast.21, bf16[8,96,128]{2,1,0:T(8,128)(2,1)S(1)} %bitcast.23), custom_call_target="tpu_custom_call" | custom-call | bytes 12000000 | tf_op jit(solution)/shard_map/square_blocks/pallas_call | solution.py:85
  19.5 0.0 collective-permute-done.g0_ref
  19.5 0.0 collective-permute-done.1.g1_ref
  19.5 0.0 collective-permute-done.2.g2_ref
  19.5 0.0 collective-permute-done.3.g3_ref
  19.5 0.0 copy-done.7
  19.6 0.0 copy-done.6
  19.6 0.0 copy-done.3
  19.6 0.0 copy-done.4
  19.6 6.9 %make_terms.1 = bf16[32,200,128]{2,1,0:T(8,128)(2,1)S(1)} custom-call(s32[8,27]{1,0:T(8,128)S(1)} %bitcast.26, s32[8]{0:T(128)S(1)} %bitcast.28, s32[8,2,27]{2,1,0:T(2,128)S(1)} %bitcast.25, s32[16]{0:T(128)S(1)} %bitcast.29, s32[3,1,16]{2,1,0:T(1,128)S(1)} %copy.9.dest_ref, bf16[8,96,3456]{2,1,0:T(8,128)(2,1)S(1)} %get-tuple-element.11.square_ref, ...), custom_call_target="tpu_custom_call" | custom-call | flops 1000000000 | bytes 8000000 | tf_op jit(solution)/shard_map/make_terms/pallas_call | solution.py:169
  26.5 55.9 %all_to_all.5.recv_ref = bf16[32,200,128]{2,1,0:T(8,128)(2,1)S(1)} all-to-all(bf16[32,200,128]{2,1,0:T(8,128)(2,1)S(1)} %make_terms.1), channel_id=1, replica_groups=mesh['gx'=16,'yz'=32] {'yz'}, dimensions={0} | all-to-all | bytes 3276800 | tf_op jit(solution)/shard_map/all_to_all | solution.py:257
  82.3 3.0 %sum_terms.1 = f32[48,4096]{1,0:T(8,128)} custom-call(bf16[32,200,128]{2,1,0:T(8,128)(2,1)S(1)} %all_to_all.5.recv_ref), custom_call_target="tpu_custom_call" | custom-call | tf_op jit(solution)/shard_map/sum_terms/pallas_call | solution.py:222
  (1 shorter events, 0.0 us)
Async XLA Ops:
  0.0 19.6 %copy-start.7 = (s32[1,1,16,1]{2,3,1,0:T(1,128)S(1)}, s32[1,1,16,1]{2,3,1,0:T(1,128)}, u32[]{:S(2)}) copy-start(s32[1,1,16,1]{2,3,1,0:T(1,128)} %param.14) | copy-start | bytes 196
  0.0 19.6 %copy-start.6 = (s32[1,1,8]{2,1,0:T(1,128)S(1)}, s32[1,1,8]{2,1,0:T(1,128)}, u32[]{:S(2)}) copy-start(s32[1,1,8]{2,1,0:T(1,128)} %param.11) | copy-start | bytes 100
  0.0 1.0 %copy-start.1 = (bf16[1,1,8,96,128]{4,3,2,1,0:T(8,128)(2,1)S(1)}, bf16[1,1,8,96,128]{4,3,2,1,0:T(8,128)(2,1)}, u32[]{:S(2)}) copy-start(bf16[1,1,8,96,128]{4,3,2,1,0:T(8,128)(2,1)} %param.9) | copy-start | bytes 589828
  1.0 0.7 copy-start.5
  1.6 17.9 %copy-start.3 = (s32[1,1,8,27,2]{3,4,2,1,0:T(2,128)S(1)}, s32[1,1,8,27,2]{3,4,2,1,0:T(2,128)}, u32[]{:S(2)}) copy-start(s32[1,1,8,27,2]{3,4,2,1,0:T(2,128)} %param.12) | copy-start | bytes 5188
  1.6 17.9 %copy-start.4 = (s32[1,1,8,27]{3,2,1,0:T(8,128)S(1)}, s32[1,1,8,27]{3,2,1,0:T(8,128)}, u32[]{:S(2)}) copy-start(s32[1,1,8,27]{3,2,1,0:T(8,128)} %param.10) | copy-start | bytes 2596
  2.2 17.3 %collective-permute-start = (bf16[2,96,128]{2,1,0:T(8,128)(2,1)S(1)}, bf16[2,96,128]{2,1,0:T(8,128)(2,1)S(1)}, u32[]{:S(2)}, u32[]{:S(2)}) collective-permute-start(bf16[2,96,128]{2,1,0:T(8,128)(2,1)S(1)} %get-tuple-element.13), channel_id=1, source_target_pairs={{0,32},{32,64},{64,96},{96,128},{128,160},{160,192},{192,224},{224... | collective-permute-start | bytes 147464 | tf_op jit(solution)/shard_map/ppermute | solution.py:246
  4.1 15.4 %collective-permute-start.1 = (bf16[2,96,128]{2,1,0:T(8,128)(2,1)S(1)}, bf16[2,96,128]{2,1,0:T(8,128)(2,1)S(1)}, u32[]{:S(2)}, u32[]{:S(2)}) collective-permute-start(bf16[2,96,128]{2,1,0:T(8,128)(2,1)S(1)} %get-tuple-element.14), channel_id=1, source_target_pairs={{32,0},{64,32},{96,64},{128,96},{160,128},{192,160},{224,192},{256... | collective-permute-start | bytes 147464 | tf_op jit(solution)/shard_map/ppermute | solution.py:247
  7.8 11.7 %collective-permute-start.2 = (bf16[2,96,128]{2,1,0:T(8,128)(2,1)S(1)}, bf16[2,96,128]{2,1,0:T(8,128)(2,1)S(1)}, u32[]{:S(2)}, u32[]{:S(2)}) collective-permute-start(bf16[2,96,128]{2,1,0:T(8,128)(2,1)S(1)} %get-tuple-element.15), channel_id=1, source_target_pairs={{0,1},{1,2},{2,3},{3,4},{4,5},{5,6},{6,7},{7,8},{8,9},{9,10},{10,1... | collective-permute-start | bytes 147464 | tf_op jit(solution)/shard_map/ppermute | solution.py:246
  12.1 7.5 %collective-permute-start.3 = (bf16[2,96,128]{2,1,0:T(8,128)(2,1)S(1)}, bf16[2,96,128]{2,1,0:T(8,128)(2,1)S(1)}, u32[]{:S(2)}, u32[]{:S(2)}) collective-permute-start(bf16[2,96,128]{2,1,0:T(8,128)(2,1)S(1)} %get-tuple-element.16), channel_id=1, source_target_pairs={{1,0},{2,1},{3,2},{4,3},{5,4},{6,5},{7,6},{8,7},{9,8},{10,9},{11,1... | collective-permute-start | bytes 147464 | tf_op jit(solution)/shard_map/ppermute | solution.py:247
  14.1 2.1 %copy-start = (bf16[1,1,8,27,9216]{4,2,3,1,0:T(8,128)(2,1)S(1)}, bf16[1,1,8,27,9216]{4,2,3,1,0:T(8,128)(2,1)}, u32[]{:S(2)}) copy-start(bf16[1,1,8,27,9216]{4,2,3,1,0:T(8,128)(2,1)} %param.8) | copy-start | bytes 11943940
  16.2 0.9 %copy-start.2 = (bf16[1,1,8,96,128]{4,3,2,1,0:T(8,128)(2,1)S(1)}, bf16[1,1,8,96,128]{4,3,2,1,0:T(8,128)(2,1)}, u32[]{:S(2)}) copy-start(bf16[1,1,8,96,128]{4,3,2,1,0:T(8,128)(2,1)} %param.9) | copy-start | bytes 589828

commit v2 on v1

v2 whole, which is shorter than its diff:
```python
import functools
import jax
import jax.numpy as jnp
from jax import lax
from jax.experimental import pallas as pl
from jax.experimental.pallas import tpu as pltpu
from jax.sharding import PartitionSpec as P

BK = 96
BP = 64
KW = 27
PW = 2
QW = 3
NB = 8
G = 2
EXT = NB + 4 * G
M = NB * PW
NS = 48
LANES = 128
TERMS = M * QW
PIECES = BP * BP // LANES
SEND_ROWS = TERMS + 8
FLAT_PARTS = ((0, 6), (6, 9), (15, 12))
SUM_OWNERS = 4
VMEM_LIMIT = 20 * 1024 * 1024


def pick_kernel(glist_hbm, prolong_hbm, *refs):
    out_refs, (glist_ref, prolong_ref, sem) = refs[:4], refs[4:]
    copies = [
        pltpu.make_async_copy(glist_hbm, glist_ref, sem.at[0]),
        pltpu.make_async_copy(prolong_hbm, prolong_ref, sem.at[1]),
    ]
    for copy in copies:
        copy.start()
    for copy in copies:
        copy.wait()
    for side, out_ref in enumerate(out_refs):
        for n in range(G):
            out_ref[n] = prolong_ref[glist_ref[n, side]]


def pick_rows(glist, prolong):
    piece = jax.ShapeDtypeStruct((G, BK, PW * BP), jnp.bfloat16)
    return pl.pallas_call(
        pick_kernel,
        out_shape=[piece] * 4,
        in_specs=[pl.BlockSpec(memory_space=pltpu.HBM)] * 2,
        out_specs=[pl.BlockSpec(memory_space=pltpu.VMEM)] * 4,
        scratch_shapes=[
            pltpu.SMEM((G, 4), jnp.int32),
            pltpu.VMEM((NB, BK, PW * BP), jnp.bfloat16),
            pltpu.SemaphoreType.DMA((2,)),
        ],
        compiler_params=pltpu.CompilerParams(vmem_limit_bytes=VMEM_LIMIT),
        name="pick_rows",
    )(*(pltpu.with_memory_space_constraint(x, pltpu.HBM) for x in (glist, prolong)))


def square_kernel(
    flat_hbm, prolong_hbm, out_ref, turned_ref, prolong_ref, flat_ref, spread_ref, flat_sem, sem
):
    flat_copies = [
        pltpu.make_async_copy(flat_hbm.at[t : t + n], flat_ref.at[t : t + n], flat_sem.at[part])
        for part, (t, n) in enumerate(FLAT_PARTS)
    ]
    prolong_copy = pltpu.make_async_copy(prolong_hbm, prolong_ref, sem)
    prolong_copy.start()
    for copy in flat_copies:
        copy.start()
    prolong_copy.wait()
    r_from = lax.broadcasted_iota(jnp.int32, (BK, BK), 0)
    r_to = lax.broadcasted_iota(jnp.int32, (BK, BK), 1)
    row_order = (r_from == (r_to % (BK // 4)) * 4 + r_to // (BK // 4)).astype(jnp.bfloat16)
    c_to = lax.broadcasted_iota(jnp.int32, (LANES, LANES), 0)
    c_from = lax.broadcasted_iota(jnp.int32, (LANES, LANES), 1)
    in_pair = c_to % BP
    column_order = (
        c_from == c_to // BP * BP + (in_pair % (BP // 2)) * 2 + in_pair // (BP // 2)
    ).astype(jnp.bfloat16)
    for i in range(NB):
        turned = lax.dot_general(
            column_order, prolong_ref[i], (((1,), (1,)), ((), ())),
            preferred_element_type=jnp.float32,
        ).astype(jnp.bfloat16)
        turned_ref[i] = jnp.dot(
            turned, row_order, preferred_element_type=jnp.float32
        ).astype(jnp.bfloat16)
    lane = lax.broadcasted_iota(jnp.int32, (BK // 4, LANES), 1)
    for t in range(KW):
        for part, (first, _) in enumerate(FLAT_PARTS):
            if t == first:
                flat_copies[part].wait()
        for c in range(BK * BK // LANES):
            spread_ref[t % 2, c * NB : (c + 1) * NB, :] = flat_ref[
                t, :, c * LANES : (c + 1) * LANES
            ].astype(jnp.float32)
        for i in range(NB):
            v0, v1, v2 = (
                spread_ref[t % 2, pl.ds(u * NB + i, BK // 4, stride=3 * NB), :] for u in range(3)
            )
            rows = [
                v0,
                pltpu.roll(jnp.where(lane >= 96, v0, v1), 32, 1),
                pltpu.roll(jnp.where(lane >= 64, v1, v2), 64, 1),
                pltpu.roll(v2, 96, 1),
            ]
            out_ref[i, :, t * LANES : (t + 1) * LANES] = jnp.concatenate(rows, 0).astype(
                jnp.bfloat16
            )


def square_blocks(flat, prolong):
    vmem = pl.BlockSpec(memory_space=pltpu.VMEM)
    return pl.pallas_call(
        square_kernel,
        out_shape=[
            jax.ShapeDtypeStruct((NB, BK, KW * LANES), jnp.bfloat16),
            jax.ShapeDtypeStruct((NB, LANES, BK), jnp.bfloat16),
            jax.ShapeDtypeStruct((NB, BK, LANES), jnp.bfloat16),
        ],
        in_specs=[pl.BlockSpec(memory_space=pltpu.HBM)] * 2,
        out_specs=[vmem] * 3,
        scratch_shapes=[
            pltpu.VMEM((KW, NB, BK * BK), jnp.bfloat16),
            pltpu.VMEM((2, BK * BK // LANES * NB, LANES), jnp.float32),
            pltpu.SemaphoreType.DMA((len(FLAT_PARTS),)),
            pltpu.SemaphoreType.DMA,
        ],
        compiler_params=pltpu.CompilerParams(vmem_limit_bytes=VMEM_LIMIT),
        cost_estimate=pl.CostEstimate(flops=0, bytes_accessed=12_000_000, transcendentals=0),
        name="square_blocks",
    )(*(pltpu.with_memory_space_constraint(x, pltpu.HBM) for x in (flat, prolong)))


def terms_kernel(
    kcol_hbm, kcount_hbm, qslot_hbm, owner_hbm, dest_hbm,
    square_ref, turned_ref, prolong_ref, g0_ref, g1_ref, g2_ref, g3_ref,
    send_ref,
    ext_ref, terms_ref, kcol_ref, kcount_ref, qslot_ref, owner_ref, dest_ref, sem,
):
    copies = [
        pltpu.make_async_copy(source, target, sem.at[n])
        for n, (source, target) in enumerate(
            (
                (kcol_hbm, kcol_ref),
                (kcount_hbm, kcount_ref),
                (qslot_hbm, qslot_ref),
                (owner_hbm, owner_ref),
                (dest_hbm, dest_ref),
            )
        )
    ]
    for copy in copies:
        copy.start()
    lane = lax.broadcasted_iota(jnp.int32, (1, LANES), 1)
    left = lane < BP
    ext_ref[:NB] = prolong_ref[...]
    for n, ghost_ref in enumerate((g0_ref, g1_ref, g2_ref, g3_ref)):
        ext_ref[NB + n * G : NB + (n + 1) * G] = ghost_ref[...]

    for copy in copies:
        copy.wait()

    def one_row(i, carry):
        live = kcount_ref[i]
        merged = [jnp.zeros((BK, LANES), jnp.float32) for _ in range(QW)]
        for t in range(KW):
            q0 = jnp.where(t < live, qslot_ref[i, 0, t], QW)
            q1 = jnp.where(t < live, qslot_ref[i, 1, t], QW)
            product = jnp.dot(
                square_ref[i, :, t * LANES : t * LANES + BK],
                ext_ref[kcol_ref[i, t]],
                preferred_element_type=jnp.float32,
            )
            column = jnp.where(left, q0, q1)
            for q in range(QW):
                merged[q] += jnp.where(column == q, product, 0.0)
        merged = [part + pltpu.roll(part, BP, 1) for part in merged]
        merged = jnp.concatenate([jnp.where(left, merged[0], merged[1]), merged[2]], 1)
        terms = jnp.dot(
            turned_ref[i], merged.astype(jnp.bfloat16), preferred_element_type=jnp.float32
        )
        for a in range(PW):
            even = terms[a * BP : a * BP + BP // 2]
            odd = terms[a * BP + BP // 2 : (a + 1) * BP]
            even_01, even_2 = even[:, :LANES], even[:, LANES:]
            odd_01, odd_2 = odd[:, :LANES], odd[:, LANES:]
            tiles = [
                jnp.where(left, even_01, pltpu.roll(odd_01, BP, 1)),
                jnp.where(left, pltpu.roll(even_01, BP, 1), odd_01),
                jnp.where(left, even_2, odd_2),
            ]
            start = pl.multiple_of((i * PW + a) * QW * PIECES, QW * PIECES)
            terms_ref[pl.ds(start, QW * PIECES), :] = jnp.concatenate(tiles, 0)
        return carry

    lax.fori_loop(0, NB, one_row, 0)
    row = lax.broadcasted_iota(jnp.int32, (8, LANES), 0)
    labels = jnp.zeros((8, LANES), jnp.float32)
    for m in range(M):
        owner = owner_ref[m].astype(jnp.float32)
        for q in range(QW):
            pair = jnp.where(row == 0, owner, dest_ref[0, q, 0, m].astype(jnp.float32))
            labels = jnp.where(lane == m * QW + q, pair, labels)
    labels = labels.astype(jnp.bfloat16)
    for piece in range(PIECES):
        send_ref[piece, :TERMS, :] = jnp.concatenate(
            [
                terms_ref[pl.ds(n * PIECES + piece, 8, stride=PIECES), :]
                for n in range(0, TERMS, 8)
            ],
            0,
        ).astype(jnp.bfloat16)
        send_ref[piece, TERMS:, :] = labels


def make_terms(kcol, kcount, qslot, owner, dest, squares, turned, prolong, ghosts):
    hbm = pl.BlockSpec(memory_space=pltpu.HBM)
    vmem = pl.BlockSpec(memory_space=pltpu.VMEM)
    numbers = [
        pltpu.with_memory_space_constraint(x, pltpu.HBM)
        for x in (kcol, kcount, qslot, owner, dest)
    ]
    return pl.pallas_call(
        terms_kernel,
        out_shape=jax.ShapeDtypeStruct((PIECES, SEND_ROWS, LANES), jnp.bfloat16),
        in_specs=[hbm] * 5 + [vmem] * 7,
        out_specs=vmem,
        scratch_shapes=[
            pltpu.VMEM((EXT, BK, LANES), jnp.bfloat16),
            pltpu.VMEM((TERMS * PIECES, LANES), jnp.float32),
            *(pltpu.SMEM(x.shape, jnp.int32) for x in numbers),
            pltpu.SemaphoreType.DMA((5,)),
        ],
        compiler_params=pltpu.CompilerParams(vmem_limit_bytes=VMEM_LIMIT),
        cost_estimate=pl.CostEstimate(
            flops=1_000_000_000, bytes_accessed=8_000_000, transcendentals=0
        ),
        name="make_terms",
    )(*numbers, squares, turned, prolong, *ghosts)


def sum_kernel(recv_ref, send_ref, value_ref, slot_ref, owner_ref):
    sources, owners = recv_ref.shape[0], send_ref.shape[0]
    width = sources * TERMS
    lane = lax.broadcasted_iota(jnp.int32, (8, LANES), 1)
    tiles = [None] * (width // LANES)
    for s in range(sources):
        value_ref[s * TERMS : (s + 1) * TERMS, :] = recv_ref[s, :TERMS, :]
        labels = recv_ref[s, TERMS:, :].astype(jnp.float32)
        n, start = divmod(s * TERMS, LANES)
        if start:
            labels = pltpu.roll(labels, start, 1)
            tiles[n] = jnp.where(lane >= start, labels, tiles[n])
            if start + TERMS > LANES:
                tiles[n + 1] = labels
        else:
            tiles[n] = labels
    slot = lax.broadcasted_iota(jnp.int32, (NS, LANES), 0).astype(jnp.float32)
    for n, tile in enumerate(tiles):
        at = slice(n * LANES, (n + 1) * LANES)
        owner_ref[:, at] = jnp.broadcast_to(tile[0:1], (16, LANES)).astype(jnp.bfloat16)
        slot_ref[:, at] = (slot == tile[1:2]).astype(jnp.bfloat16)
    values = value_ref[...]
    for o in range(0, owners, SUM_OWNERS):
        chosen = []
        for this in range(o, o + SUM_OWNERS):
            here = jnp.where(owner_ref[...] == this, 1.0, 0.0).astype(jnp.bfloat16)
            chosen += [slot_ref[r : r + 16, :] * here for r in range(0, NS, 16)]
        sums = jnp.dot(
            jnp.concatenate(chosen, 0), values, preferred_element_type=jnp.float32
        ).astype(jnp.bfloat16)
        for n in range(SUM_OWNERS):
            send_ref[o + n] = sums[n * NS : (n + 1) * NS]


def sum_terms(received):
    sources = received.shape[0]
    vmem = pl.BlockSpec(memory_space=pltpu.VMEM)
    return pl.pallas_call(
        sum_kernel,
        out_shape=jax.ShapeDtypeStruct((sources, NS, LANES), jnp.bfloat16),
        in_specs=[vmem],
        out_specs=vmem,
        scratch_shapes=[
            pltpu.VMEM((sources * TERMS, LANES), jnp.bfloat16),
            pltpu.VMEM((NS, sources * TERMS), jnp.bfloat16),
            pltpu.VMEM((16, sources * TERMS), jnp.bfloat16),
        ],
        compiler_params=pltpu.CompilerParams(vmem_limit_bytes=VMEM_LIMIT),
        name="sum_terms",
    )(received)


def join_kernel(recv_ref, out_ref):
    for piece in range(PIECES):
        out_ref[:, piece * LANES : (piece + 1) * LANES] = recv_ref[piece].astype(jnp.float32)


def join_pieces(received):
    vmem = pl.BlockSpec(memory_space=pltpu.VMEM)
    return pl.pallas_call(
        join_kernel,
        out_shape=jax.ShapeDtypeStruct((NS, BP * BP), jnp.float32),
        in_specs=[vmem],
        out_specs=vmem,
        compiler_params=pltpu.CompilerParams(vmem_limit_bytes=VMEM_LIMIT),
        name="join_pieces",
    )(received)


def on_device(stiffness, prolong, kcol, kcount, qslot, glist, owner, dest):
    prolong_rows = prolong[0, 0]
    picked = pick_rows(jnp.transpose(glist[0, 0]), prolong_rows)
    ghosts = []
    for axis, to_lower, to_upper in (("gx", 0, 1), ("yz", 2, 3)):
        size = lax.axis_size(axis)
        up = [(n, n + 1) for n in range(size - 1)]
        down = [(n + 1, n) for n in range(size - 1)]
        ghosts.append(lax.ppermute(picked[to_upper], axis, up))
        ghosts.append(lax.ppermute(picked[to_lower], axis, down))
    squares, turned, own_rows = square_blocks(jnp.transpose(stiffness[0, 0], (1, 0, 2)), prolong_rows)
    packed = make_terms(
        kcol[0, 0],
        kcount[0, 0],
        jnp.transpose(qslot[0, 0], (0, 2, 1)),
        owner[0, 0, :, 0],
        jnp.transpose(dest, (0, 3, 1, 2)),
        squares, turned, own_rows, ghosts,
    )
    received = lax.all_to_all(packed, "yz", split_axis=0, concat_axis=0, tiled=True)
    pieces = lax.all_to_all(sum_terms(received), "yz", split_axis=0, concat_axis=0, tiled=True)
    return join_pieces(pieces)[None, None]


def solution(mesh):
    split = ("gx", "yz")
    in_specs = tuple(P(*split, *(None,) * n) for n in (3, 3, 2, 1, 3, 2, 2, 2))
    return jax.shard_map(
        on_device, mesh=mesh, in_specs=in_specs, out_specs=P(*split, None, None), check_vma=False
    )
```

time: 85.7 us -> 77.9 us (0.909)
  the two profiles are of different devices: /device:TPU:24 before, /device:TPU:88 now
where the time goes in v2:
time: 77.9 us; the launch traced here: 77.5 us
  blocking collectives  49.5 us (64%)
  Pallas kernels  16.1 us (21%)
  starting transfers between devices  11.8 us (15%)
    all_to_all x1, blocking collectives, on_device(): lax.all_to_all(packed, 'yz', split_axis=0, concat_axis=0, tiled=True)  30.2 us
    all_to_all x1, blocking collectives, on_device(): lax.all_to_all(sum_terms(received), 'yz', split_axis=0, concat_axis=0, ti...  19.3 us
    pallas_call x1, Pallas kernels, make_terms(): pl.pallas_call(terms_kernel, out_shape=jax.ShapeDtypeStruct((PIECES, SEND...  7.5 us
    ppermute x2, starting transfers between devices, on_device(): ghosts.append(lax.ppermute(picked[to_upper], axis, up))  6.2 us
    ppermute x2, starting transfers between devices, on_device(): ghosts.append(lax.ppermute(picked[to_lower], axis, down))  5.56 us
    pallas_call x1, Pallas kernels, square_blocks(): pl.pallas_call(square_kernel, out_shape=[jax.ShapeDtypeStruct((NB, BK, KW...  5.2 us
  transfers between devices with their start and end apart: 4, of which 0 were waited for; matrix products, arithmetic and copies ran while one was open for 0% of the time, Pallas kernels for 7%

profile of v2, /device:TPU:88, one launch (start us, length us, event | category | flops | bytes accessed | tf_op | source)
XLA Modules:
  0.0 77.5 jit_solution(3890553269425671079)
XLA Ops:
  0.0 1.0 %pick_rows.1 = (bf16[2,96,128]{2,1,0:T(8,128)(2,1)S(1)}, bf16[2,96,128]{2,1,0:T(8,128)(2,1)S(1)}, bf16[2,96,128]{2,1,0:T(8,128)(2,1)S(1)}, bf16[2,96,128]{2,1,0:T(8,128)(2,1)S(1)}) custom-call(s32[2,4]{1,0:T(2,128)} %bitcast.21, bf16[8,96,128]{2,1,0:T(8,128)(2,1)} %bitcast.16), custom_call_target="tpu_custom_call" | custom-call | tf_op jit(solution)/shard_map/pick_rows/pallas_call | solution.py:45
  1.0 1.9 %collective-permute-start = (bf16[2,96,128]{2,1,0:T(8,128)(2,1)S(1)}, bf16[2,96,128]{2,1,0:T(8,128)(2,1)S(1)}, u32[]{:S(2)}, u32[]{:S(2)}) collective-permute-start(bf16[2,96,128]{2,1,0:T(8,128)(2,1)S(1)} %get-tuple-element.15), channel_id=1, source_target_pairs={{0,32},{32,64},{64,96},{96,128},{128,160},{160,192},{192,224},{224... | collective-permute-start | bytes 147464 | tf_op jit(solution)/shard_map/ppermute | solution.py:321
  2.9 3.6 %collective-permute-start.1 = (bf16[2,96,128]{2,1,0:T(8,128)(2,1)S(1)}, bf16[2,96,128]{2,1,0:T(8,128)(2,1)S(1)}, u32[]{:S(2)}, u32[]{:S(2)}) collective-permute-start(bf16[2,96,128]{2,1,0:T(8,128)(2,1)S(1)} %get-tuple-element.16), channel_id=1, source_target_pairs={{32,0},{64,32},{96,64},{128,96},{160,128},{192,160},{224,192},{256... | collective-permute-start | bytes 147464 | tf_op jit(solution)/shard_map/ppermute | solution.py:322
  6.5 4.3 %collective-permute-start.2 = (bf16[2,96,128]{2,1,0:T(8,128)(2,1)S(1)}, bf16[2,96,128]{2,1,0:T(8,128)(2,1)S(1)}, u32[]{:S(2)}, u32[]{:S(2)}) collective-permute-start(bf16[2,96,128]{2,1,0:T(8,128)(2,1)S(1)} %get-tuple-element.17), channel_id=1, source_target_pairs={{0,1},{1,2},{2,3},{3,4},{4,5},{5,6},{6,7},{7,8},{8,9},{9,10},{10,1... | collective-permute-start | bytes 147464 | tf_op jit(solution)/shard_map/ppermute | solution.py:321
  10.8 1.9 %collective-permute-start.3 = (bf16[2,96,128]{2,1,0:T(8,128)(2,1)S(1)}, bf16[2,96,128]{2,1,0:T(8,128)(2,1)S(1)}, u32[]{:S(2)}, u32[]{:S(2)}) collective-permute-start(bf16[2,96,128]{2,1,0:T(8,128)(2,1)S(1)} %get-tuple-element.18), channel_id=1, source_target_pairs={{1,0},{2,1},{3,2},{4,3},{5,4},{6,5},{7,6},{8,7},{9,8},{10,9},{11,1... | collective-permute-start | bytes 147464 | tf_op jit(solution)/shard_map/ppermute | solution.py:322
  12.8 5.2 %square_blocks.1 = (bf16[8,96,3456]{2,1,0:T(8,128)(2,1)S(1)}, bf16[8,128,96]{2,1,0:T(8,128)(2,1)S(1)}, bf16[8,96,128]{2,1,0:T(8,128)(2,1)S(1)}) custom-call(bf16[27,8,9216]{2,1,0:T(8,128)(2,1)} %bitcast.15, bf16[8,96,128]{2,1,0:T(8,128)(2,1)} %bitcast.17), custom_call_target="tpu_custom_call" | custom-call | bytes 12000000 | tf_op jit(solution)/shard_map/square_blocks/pallas_call | solution.py:115
  18.0 0.0 collective-permute-done.g0_ref
  18.0 0.0 collective-permute-done.1.g1_ref
  18.0 0.0 collective-permute-done.2.g2_ref
  18.0 0.0 collective-permute-done.3.g3_ref
  18.0 7.5 %make_terms.1 = bf16[32,56,128]{2,1,0:T(8,128)(2,1)S(1)} custom-call(s32[8,27]{1,0:T(8,128)} %bitcast.19, s32[8]{0:T(128)} %bitcast.22, s32[8,2,27]{2,1,0:T(2,128)} %bitcast.18, s32[16]{0:T(128)} %bitcast.23, s32[1,3,1,16]{3,2,1,0:T(1,128)} %bitcast.20, bf16[8,96,3456]{2,1,0:T(8,128)(2,1)S(1)} %get-tuple-element.12.square_ref, ...), custom_call_target="tpu_custom_call" | custom-call | flops 1000000000 | bytes 8000000 | tf_op jit(solution)/shard_map/make_terms/pallas_call | solution.py:225
  25.5 30.2 %all_to_all.10.recv_ref = bf16[32,56,128]{2,1,0:T(8,128)(2,1)S(1)} all-to-all(bf16[32,56,128]{2,1,0:T(8,128)(2,1)S(1)} %make_terms.1), channel_id=1, replica_groups=mesh['gx'=16,'yz'=32] {'yz'}, dimensions={0} | all-to-all | bytes 917504 | tf_op jit(solution)/shard_map/all_to_all | solution.py:332
  55.7 1.5 %sum_terms.1 = bf16[32,48,128]{2,1,0:T(8,128)(2,1)S(1)} custom-call(bf16[32,56,128]{2,1,0:T(8,128)(2,1)S(1)} %all_to_all.10.recv_ref), custom_call_target="tpu_custom_call" | custom-call | tf_op jit(solution)/shard_map/sum_terms/pallas_call | solution.py:281
  57.2 19.3 %all_to_all.11.recv_ref = bf16[32,48,128]{2,1,0:T(8,128)(2,1)S(1)} all-to-all(bf16[32,48,128]{2,1,0:T(8,128)(2,1)S(1)} %sum_terms.1), channel_id=1, replica_groups=mesh['gx'=16,'yz'=32] {'yz'}, dimensions={0} | all-to-all | bytes 786432 | tf_op jit(solution)/shard_map/all_to_all | solution.py:333
  76.5 0.9 %join_pieces.1 = f32[48,4096]{1,0:T(8,128)} custom-call(bf16[32,48,128]{2,1,0:T(8,128)(2,1)S(1)} %all_to_all.11.recv_ref), custom_call_target="tpu_custom_call" | custom-call | tf_op jit(solution)/shard_map/join_pieces/pallas_call | solution.py:303
Async XLA Ops:
  1.0 17.0 %collective-permute-start = (bf16[2,96,128]{2,1,0:T(8,128)(2,1)S(1)}, bf16[2,96,128]{2,1,0:T(8,128)(2,1)S(1)}, u32[]{:S(2)}, u32[]{:S(2)}) collective-permute-start(bf16[2,96,128]{2,1,0:T(8,128)(2,1)S(1)} %get-tuple-element.15), channel_id=1, source_target_pairs={{0,32},{32,64},{64,96},{96,128},{128,160},{160,192},{192,224},{224... | collective-permute-start | bytes 147464 | tf_op jit(solution)/shard_map/ppermute | solution.py:321
  2.9 15.1 %collective-permute-start.1 = (bf16[2,96,128]{2,1,0:T(8,128)(2,1)S(1)}, bf16[2,96,128]{2,1,0:T(8,128)(2,1)S(1)}, u32[]{:S(2)}, u32[]{:S(2)}) collective-permute-start(bf16[2,96,128]{2,1,0:T(8,128)(2,1)S(1)} %get-tuple-element.16), channel_id=1, source_target_pairs={{32,0},{64,32},{96,64},{128,96},{160,128},{192,160},{224,192},{256... | collective-permute-start | bytes 147464 | tf_op jit(solution)/shard_map/ppermute | solution.py:322
  6.5 11.4 %collective-permute-start.2 = (bf16[2,96,128]{2,1,0:T(8,128)(2,1)S(1)}, bf16[2,96,128]{2,1,0:T(8,128)(2,1)S(1)}, u32[]{:S(2)}, u32[]{:S(2)}) collective-permute-start(bf16[2,96,128]{2,1,0:T(8,128)(2,1)S(1)} %get-tuple-element.17), channel_id=1, source_target_pairs={{0,1},{1,2},{2,3},{3,4},{4,5},{5,6},{6,7},{7,8},{8,9},{9,10},{10,1... | collective-permute-start | bytes 147464 | tf_op jit(solution)/shard_map/ppermute | solution.py:321
  10.8 7.2 %collective-permute-start.3 = (bf16[2,96,128]{2,1,0:T(8,128)(2,1)S(1)}, bf16[2,96,128]{2,1,0:T(8,128)(2,1)S(1)}, u32[]{:S(2)}, u32[]{:S(2)}) collective-permute-start(bf16[2,96,128]{2,1,0:T(8,128)(2,1)S(1)} %get-tuple-element.18), channel_id=1, source_target_pairs={{1,0},{2,1},{3,2},{4,3},{5,4},{6,5},{7,6},{8,7},{9,8},{10,9},{11,1... | collective-permute-start | bytes 147464 | tf_op jit(solution)/shard_map/ppermute | solution.py:322

commit v3 on v2

--- a/solution.py
+++ b/solution.py
@@ -20,9 +20,25 @@
 TERMS = M * QW
 PIECES = BP * BP // LANES
 SEND_ROWS = TERMS + 8
-FLAT_PARTS = ((0, 6), (6, 9), (15, 12))
+FLAT_PARTS = ((0, 9), (9, 18), (18, 24), (24, 27))
+UNROLL = 3
 SUM_OWNERS = 4
 VMEM_LIMIT = 20 * 1024 * 1024
+
+
+def parity(axis):
+    return lax.rem(lax.axis_index(axis), 2)
+
+
+def side_of(swap):
+    odd = parity("gx" if swap < 2 else "yz")
+    return swap // 2 * 2 + (odd if swap % 2 else 1 - odd)
+
+
+def swap_pairs(swap, size):
+    first = swap % 2
+    pairs = [(n, n + 1) for n in range(first, size - 1, 2)]
+    return pairs + [(j, i) for i, j in pairs]
 
 
 def pick_kernel(glist_hbm, prolong_hbm, *refs):
@@ -35,9 +51,9 @@
         copy.start()
     for copy in copies:
         copy.wait()
-    for side, out_ref in enumerate(out_refs):
+    for swap, out_ref in enumerate(out_refs):
         for n in range(G):
-            out_ref[n] = prolong_ref[glist_ref[n, side]]
+            out_ref[n] = prolong_ref[glist_ref[n, side_of(swap)]]
 
 
 def pick_rows(glist, prolong):
@@ -57,18 +73,7 @@
     )(*(pltpu.with_memory_space_constraint(x, pltpu.HBM) for x in (glist, prolong)))
 
 
-def square_kernel(
-    flat_hbm, prolong_hbm, out_ref, turned_ref, prolong_ref, flat_ref, spread_ref, flat_sem, sem
-):
-    flat_copies = [
-        pltpu.make_async_copy(flat_hbm.at[t : t + n], flat_ref.at[t : t + n], flat_sem.at[part])
-        for part, (t, n) in enumerate(FLAT_PARTS)
-    ]
-    prolong_copy = pltpu.make_async_copy(prolong_hbm, prolong_ref, sem)
-    prolong_copy.start()
-    for copy in flat_copies:
-        copy.start()
-    prolong_copy.wait()
+def turn_rows(prolong_ref, turned_ref):
     r_from = lax.broadcasted_iota(jnp.int32, (BK, BK), 0)
     r_to = lax.broadcasted_iota(jnp.int32, (BK, BK), 1)
     row_order = (r_from == (r_to % (BK // 4)) * 4 + r_to // (BK // 4)).astype(jnp.bfloat16)
@@ -86,60 +91,66 @@
         turned_ref[i] = jnp.dot(
             turned, row_order, preferred_element_type=jnp.float32
         ).astype(jnp.bfloat16)
-    lane = lax.broadcasted_iota(jnp.int32, (BK // 4, LANES), 1)
-    for t in range(KW):
-        for part, (first, _) in enumerate(FLAT_PARTS):
-            if t == first:
-                flat_copies[part].wait()
-        for c in range(BK * BK // LANES):
-            spread_ref[t % 2, c * NB : (c + 1) * NB, :] = flat_ref[
-                t, :, c * LANES : (c + 1) * LANES
-            ].astype(jnp.float32)
-        for i in range(NB):
-            v0, v1, v2 = (
-                spread_ref[t % 2, pl.ds(u * NB + i, BK // 4, stride=3 * NB), :] for u in range(3)
-            )
-            rows = [
-                v0,
-                pltpu.roll(jnp.where(lane >= 96, v0, v1), 32, 1),
-                pltpu.roll(jnp.where(lane >= 64, v1, v2), 64, 1),
-                pltpu.roll(v2, 96, 1),
-            ]
-            out_ref[i, :, t * LANES : (t + 1) * LANES] = jnp.concatenate(rows, 0).astype(
-                jnp.bfloat16
-            )
-
-
-def square_blocks(flat, prolong):
+
+
+def spread_kernel(
+    flat_hbm, prolong_hbm, spread_ref, turned_ref, own_ref, prolong_ref, flat_ref, sem, flat_sem
+):
+    copy = pltpu.make_async_copy(prolong_hbm, prolong_ref, sem)
+    parts = [
+        pltpu.make_async_copy(flat_hbm.at[a:b], flat_ref.at[a:b], flat_sem.at[n])
+        for n, (a, b) in enumerate(FLAT_PARTS)
+    ]
+    copy.start()
+    for part in parts:
+        part.start()
+    own_ref[:, BK:, :] = jnp.zeros((NB, LANES - BK, LANES), jnp.bfloat16)
+    copy.wait()
+    own_ref[:, :BK, :] = prolong_ref[...]
+    turn_rows(prolong_ref, turned_ref)
+    for n, (a, b) in enumerate(FLAT_PARTS):
+        parts[n].wait()
+
+        def one_slot(t, carry):
+            for c in range(BK * BK // LANES):
+                spread_ref[t, c * NB : (c + 1) * NB, :] = flat_ref[
+                    t, :, c * LANES : (c + 1) * LANES
+                ].astype(jnp.float32)
+            return carry
+
+        lax.fori_loop(a, b, one_slot, 0)
+
+
+def spread_blocks(flat, prolong):
     vmem = pl.BlockSpec(memory_space=pltpu.VMEM)
     return pl.pallas_call(
-        square_kernel,
+        spread_kernel,
         out_shape=[
-            jax.ShapeDtypeStruct((NB, BK, KW * LANES), jnp.bfloat16),
+            jax.ShapeDtypeStruct((KW, BK * BK // LANES * NB, LANES), jnp.float32),
             jax.ShapeDtypeStruct((NB, LANES, BK), jnp.bfloat16),
-            jax.ShapeDtypeStruct((NB, BK, LANES), jnp.bfloat16),
+            jax.ShapeDtypeStruct((NB, LANES, LANES), jnp.bfloat16),
         ],
         in_specs=[pl.BlockSpec(memory_space=pltpu.HBM)] * 2,
         out_specs=[vmem] * 3,
         scratch_shapes=[
-            pltpu.VMEM((KW, NB, BK * BK), jnp.bfloat16),
-            pltpu.VMEM((2, BK * BK // LANES * NB, LANES), jnp.float32),
+            pltpu.VMEM(prolong.shape, jnp.bfloat16),
+            pltpu.VMEM(flat.shape, jnp.bfloat16),
+            pltpu.SemaphoreType.DMA,
             pltpu.SemaphoreType.DMA((len(FLAT_PARTS),)),
-            pltpu.SemaphoreType.DMA,
         ],
         compiler_params=pltpu.CompilerParams(vmem_limit_bytes=VMEM_LIMIT),
         cost_estimate=pl.CostEstimate(flops=0, bytes_accessed=12_000_000, transcendentals=0),
-        name="square_blocks",
+        name="spread_blocks",
     )(*(pltpu.with_memory_space_constraint(x, pltpu.HBM) for x in (flat, prolong)))
 
 
 def terms_kernel(
     kcol_hbm, kcount_hbm, qslot_hbm, owner_hbm, dest_hbm,
-    square_ref, turned_ref, prolong_ref, g0_ref, g1_ref, g2_ref, g3_ref,
+    spread_ref, turned_ref, own_ref, g0_ref, g1_ref, g2_ref, g3_ref,
     send_ref,
-    ext_ref, terms_ref, kcol_ref, kcount_ref, qslot_ref, owner_ref, dest_ref, sem,
+    kcol_ref, kcount_ref, qslot_ref, owner_ref, dest_ref, sem, ext_ref, terms_ref, *sum_refs,
 ):
-    copies = [
+    small = [
         pltpu.make_async_copy(source, target, sem.at[n])
         for n, (source, target) in enumerate(
             (
@@ -151,33 +162,60 @@
             )
         )
     ]
-    for copy in copies:
+    for copy in small:
         copy.start()
-    lane = lax.broadcasted_iota(jnp.int32, (1, LANES), 1)
-    left = lane < BP
-    ext_ref[:NB] = prolong_ref[...]
-    for n, ghost_ref in enumerate((g0_ref, g1_ref, g2_ref, g3_ref)):
-        ext_ref[NB + n * G : NB + (n + 1) * G] = ghost_ref[...]
-
-    for copy in copies:
+    for sum_ref in sum_refs:
+        sum_ref[:QW] = jnp.zeros((QW, BK, LANES), jnp.float32)
+    ext_ref[:NB] = own_ref[...]
+    ext_ref[NB:, BK:, :] = jnp.zeros((EXT - NB, LANES - BK, LANES), jnp.bfloat16)
+    for swap, ghost_ref in enumerate((g0_ref, g1_ref, g2_ref, g3_ref)):
+        ext_ref[pl.ds(NB + side_of(swap) * G, G), :BK, :] = ghost_ref[...]
+    for copy in small:
         copy.wait()
-
-    def one_row(i, carry):
-        live = kcount_ref[i]
-        merged = [jnp.zeros((BK, LANES), jnp.float32) for _ in range(QW)]
-        for t in range(KW):
-            q0 = jnp.where(t < live, qslot_ref[i, 0, t], QW)
-            q1 = jnp.where(t < live, qslot_ref[i, 1, t], QW)
+    lane = lax.broadcasted_iota(jnp.int32, (BK // 4, LANES), 1)
+
+    def one_slot(t):
+        for i in range(NB):
+            v0, v1, v2 = (
+                spread_ref[t, pl.ds(u * NB + i, BK // 4, stride=3 * NB), :] for u in range(3)
+            )
+            rows = [
+                v0,
+                pltpu.roll(jnp.where(lane >= 96, v0, v1), 32, 1),
+                pltpu.roll(jnp.where(lane >= 64, v1, v2), 64, 1),
+                pltpu.roll(v2, 96, 1),
+            ]
             product = jnp.dot(
-                square_ref[i, :, t * LANES : t * LANES + BK],
+                jnp.concatenate(rows, 0).astype(jnp.bfloat16),
                 ext_ref[kcol_ref[i, t]],
                 preferred_element_type=jnp.float32,
             )
-            column = jnp.where(left, q0, q1)
-            for q in range(QW):
-                merged[q] += jnp.where(column == q, product, 0.0)
-        merged = [part + pltpu.roll(part, BP, 1) for part in merged]
-        merged = jnp.concatenate([jnp.where(left, merged[0], merged[1]), merged[2]], 1)
+            live = t < kcount_ref[i]
+            for s in range(PW):
+                q = jnp.where(live, qslot_ref[i, s, t], QW)
+                sum_refs[i * PW + s][q] += product
+
+    def some_slots(step, carry):
+        for u in range(UNROLL):
+            one_slot(step * UNROLL + u)
+        return carry
+
+    lax.fori_loop(0, KW // UNROLL, some_slots, 0)
+
+    left = lax.broadcasted_iota(jnp.int32, (1, LANES), 1) < BP
+    for i in range(NB):
+        first, second = sum_refs[i * PW], sum_refs[i * PW + 1]
+        merged = jnp.concatenate(
+            [
+                jnp.where(
+                    left,
+                    first[0] + pltpu.roll(second[0], BP, 1),
+                    second[1] + pltpu.roll(first[1], BP, 1),
+                ),
+                first[2] + pltpu.roll(second[2], BP, 1),
+            ],
+            1,
+        )
         terms = jnp.dot(
             turned_ref[i], merged.astype(jnp.bfloat16), preferred_element_type=jnp.float32
         )
@@ -189,13 +227,11 @@
             tiles = [
                 jnp.where(left, even_01, pltpu.roll(odd_01, BP, 1)),
                 jnp.where(left, pltpu.roll(even_01, BP, 1), odd_01),
-                jnp.where(left, even_2, odd_2),
+                jnp.where(left, even_2, pltpu.roll(odd_2, BP, 1)),
             ]
-            start = pl.multiple_of((i * PW + a) * QW * PIECES, QW * PIECES)
-            terms_ref[pl.ds(start, QW * PIECES), :] = jnp.concatenate(tiles, 0)
-        return carry
-
-    lax.fori_loop(0, NB, one_row, 0)
+            start = (i * PW + a) * QW * PIECES
+            terms_ref[start : start + QW * PIECES, :] = jnp.concatenate(tiles, 0)
+    lane = lax.broadcasted_iota(jnp.int32, (1, LANES), 1)
     row = lax.broadcasted_iota(jnp.int32, (8, LANES), 0)
     labels = jnp.zeros((8, LANES), jnp.float32)
     for m in range(M):
@@ -215,7 +251,7 @@
         send_ref[piece, TERMS:, :] = labels
 
 
-def make_terms(kcol, kcount, qslot, owner, dest, squares, turned, prolong, ghosts):
+def make_terms(kcol, kcount, qslot, owner, dest, spread, turned, own, ghosts):
     hbm = pl.BlockSpec(memory_space=pltpu.HBM)
     vmem = pl.BlockSpec(memory_space=pltpu.VMEM)
     numbers = [
@@ -225,20 +261,21 @@
     return pl.pallas_call(
         terms_kernel,
         out_shape=jax.ShapeDtypeStruct((PIECES, SEND_ROWS, LANES), jnp.bfloat16),
-        in_specs=[hbm] * 5 + [vmem] * 7,
+        in_specs=[hbm] * len(numbers) + [vmem] * 7,
         out_specs=vmem,
         scratch_shapes=[
-            pltpu.VMEM((EXT, BK, LANES), jnp.bfloat16),
+            *(pltpu.SMEM(x.shape, jnp.int32) for x in numbers),
+            pltpu.SemaphoreType.DMA((len(numbers),)),
+            pltpu.VMEM((EXT, LANES, LANES), jnp.bfloat16),
             pltpu.VMEM((TERMS * PIECES, LANES), jnp.float32),
-            *(pltpu.SMEM(x.shape, jnp.int32) for x in numbers),
-            pltpu.SemaphoreType.DMA((5,)),
+            *[pltpu.VMEM((QW + 1, BK, LANES), jnp.float32)] * (NB * PW),
         ],
         compiler_params=pltpu.CompilerParams(vmem_limit_bytes=VMEM_LIMIT),
         cost_estimate=pl.CostEstimate(
             flops=1_000_000_000, bytes_accessed=8_000_000, transcendentals=0
         ),
         name="make_terms",
-    )(*numbers, squares, turned, prolong, *ghosts)
+    )(*numbers, spread, turned, own, *ghosts)
 
 
 def sum_kernel(recv_ref, send_ref, value_ref, slot_ref, owner_ref):
@@ -314,20 +351,19 @@
     prolong_rows = prolong[0, 0]
     picked = pick_rows(jnp.transpose(glist[0, 0]), prolong_rows)
     ghosts = []
-    for axis, to_lower, to_upper in (("gx", 0, 1), ("yz", 2, 3)):
-        size = lax.axis_size(axis)
-        up = [(n, n + 1) for n in range(size - 1)]
-        down = [(n + 1, n) for n in range(size - 1)]
-        ghosts.append(lax.ppermute(picked[to_upper], axis, up))
-        ghosts.append(lax.ppermute(picked[to_lower], axis, down))
-    squares, turned, own_rows = square_blocks(jnp.transpose(stiffness[0, 0], (1, 0, 2)), prolong_rows)
+    for swap, rows in enumerate(picked):
+        axis = "gx" if swap < 2 else "yz"
+        ghosts.append(lax.ppermute(rows, axis, swap_pairs(swap, lax.axis_size(axis))))
+    spread, turned, own = spread_blocks(
+        jnp.transpose(stiffness[0, 0], (1, 0, 2)), prolong_rows
+    )
     packed = make_terms(
         kcol[0, 0],
         kcount[0, 0],
         jnp.transpose(qslot[0, 0], (0, 2, 1)),
         owner[0, 0, :, 0],
         jnp.transpose(dest, (0, 3, 1, 2)),
-        squares, turned, own_rows, ghosts,
+        spread, turned, own, ghosts,
     )
     received = lax.all_to_all(packed, "yz", split_axis=0, concat_axis=0, tiled=True)
     pieces = lax.all_to_all(sum_terms(received), "yz", split_axis=0, concat_axis=0, tiled=True)

time: 77.9 us -> 74.4 us (0.955)
  Pallas kernels: 16.1 us -> 13.2 us
  blocking collectives: 49.5 us -> 47.8 us
  starting transfers between devices: 11.8 us -> 12.9 us
    all_to_all x1, blocking collectives: 30.2 us -> 27.5 us  [on_device(): lax.all_to_all(packed, 'yz', split_axis=0, concat_axis=0, tiled=True)]
    pallas_call x1, Pallas kernels: 7.5 us -> 5.97 us  [make_terms(): pl.pallas_call(terms_kernel, out_shape=jax.ShapeDtypeStruct((PIECES, SEND...]
    pallas_call x1, Pallas kernels: 5.2 us -> 3.8 us  [spread_blocks(): pl.pallas_call(spread_kernel, out_shape=[jax.ShapeDtypeStruct((KW, BK * B...]
    ppermute x4, starting transfers between devices: 11.8 us -> 12.9 us  [on_device(): lax.ppermute(rows, axis, swap_pairs(swap, lax.axis_size(axis)))]
    all_to_all x1, blocking collectives: 19.3 us -> 20.4 us  [on_device(): lax.all_to_all(sum_terms(received), 'yz', split_axis=0, concat_axis=0, ti...]
  transfers between devices with their start and end apart: 4 -> 4, of which waited for: 0 -> 0; matrix products, arithmetic and copies ran while one was open for 0% -> 0% of each run, Pallas kernels for 7% -> 5%
where the time goes in v3:
time: 74.4 us; the launch traced here: 74 us
  blocking collectives  47.8 us (64%)
  Pallas kernels  13.2 us (18%)
  starting transfers between devices  12.9 us (17%)
    all_to_all x1, blocking collectives, on_device(): lax.all_to_all(packed, 'yz', split_axis=0, concat_axis=0, tiled=True)  27.5 us
    all_to_all x1, blocking collectives, on_device(): lax.all_to_all(sum_terms(received), 'yz', split_axis=0, concat_axis=0, ti...  20.4 us
    ppermute x4, starting transfers between devices, on_device(): lax.ppermute(rows, axis, swap_pairs(swap, lax.axis_size(axis)))  12.9 us
    pallas_call x1, Pallas kernels, make_terms(): pl.pallas_call(terms_kernel, out_shape=jax.ShapeDtypeStruct((PIECES, SEND...  5.97 us
    pallas_call x1, Pallas kernels, spread_blocks(): pl.pallas_call(spread_kernel, out_shape=[jax.ShapeDtypeStruct((KW, BK * B...  3.8 us
    pallas_call x1, Pallas kernels, sum_terms(): pl.pallas_call(sum_kernel, out_shape=jax.ShapeDtypeStruct((sources, NS, L...  1.49 us
  transfers between devices with their start and end apart: 4, of which 0 were waited for; matrix products, arithmetic and copies ran while one was open for 0% of the time, Pallas kernels for 5%

profile of v3, /device:TPU:88, one launch (start us, length us, event | category | flops | bytes accessed | tf_op | source)
XLA Modules:
  0.0 74.0 jit_solution(2576377889510568832)
XLA Ops:
  0.0 1.0 %pick_rows.1 = (bf16[2,96,128]{2,1,0:T(8,128)(2,1)S(1)}, bf16[2,96,128]{2,1,0:T(8,128)(2,1)S(1)}, bf16[2,96,128]{2,1,0:T(8,128)(2,1)S(1)}, bf16[2,96,128]{2,1,0:T(8,128)(2,1)S(1)}) custom-call(s32[2,4]{1,0:T(2,128)} %bitcast.21, bf16[8,96,128]{2,1,0:T(8,128)(2,1)} %bitcast.16), custom_call_target="tpu_custom_call" | custom-call | tf_op jit(solution)/shard_map/pick_rows/pallas_call | solution.py:61
  1.0 1.9 %collective-permute-start = (bf16[2,96,128]{2,1,0:T(8,128)(2,1)S(1)}, bf16[2,96,128]{2,1,0:T(8,128)(2,1)S(1)}, u32[]{:S(2)}, u32[]{:S(2)}) collective-permute-start(bf16[2,96,128]{2,1,0:T(8,128)(2,1)S(1)} %get-tuple-element.15), channel_id=1, source_target_pairs={{0,32},{64,96},{128,160},{192,224},{256,288},{320,352},{384,416},{... | collective-permute-start | bytes 147464 | tf_op jit(solution)/shard_map/ppermute | solution.py:356
  2.9 2.5 %collective-permute-start.1 = (bf16[2,96,128]{2,1,0:T(8,128)(2,1)S(1)}, bf16[2,96,128]{2,1,0:T(8,128)(2,1)S(1)}, u32[]{:S(2)}, u32[]{:S(2)}) collective-permute-start(bf16[2,96,128]{2,1,0:T(8,128)(2,1)S(1)} %get-tuple-element.16), channel_id=1, source_target_pairs={{32,64},{96,128},{160,192},{224,256},{288,320},{352,384},{416,448}... | collective-permute-start | bytes 147464 | tf_op jit(solution)/shard_map/ppermute | solution.py:356
  5.4 1.9 %collective-permute-start.2 = (bf16[2,96,128]{2,1,0:T(8,128)(2,1)S(1)}, bf16[2,96,128]{2,1,0:T(8,128)(2,1)S(1)}, u32[]{:S(2)}, u32[]{:S(2)}) collective-permute-start(bf16[2,96,128]{2,1,0:T(8,128)(2,1)S(1)} %get-tuple-element.17), channel_id=1, source_target_pairs={{0,1},{2,3},{4,5},{6,7},{8,9},{10,11},{12,13},{14,15},{16,17},{18,... | collective-permute-start | bytes 147464 | tf_op jit(solution)/shard_map/ppermute | solution.py:356
  7.3 6.6 %collective-permute-start.3 = (bf16[2,96,128]{2,1,0:T(8,128)(2,1)S(1)}, bf16[2,96,128]{2,1,0:T(8,128)(2,1)S(1)}, u32[]{:S(2)}, u32[]{:S(2)}) collective-permute-start(bf16[2,96,128]{2,1,0:T(8,128)(2,1)S(1)} %get-tuple-element.18), channel_id=1, source_target_pairs={{1,2},{3,4},{5,6},{7,8},{9,10},{11,12},{13,14},{15,16},{17,18},{19... | collective-permute-start | bytes 147464 | tf_op jit(solution)/shard_map/ppermute | solution.py:356
  13.9 3.8 %spread_blocks.1 = (f32[27,576,128]{2,1,0:T(8,128)S(1)}, bf16[8,128,96]{2,1,0:T(8,128)(2,1)S(1)}, bf16[8,128,128]{2,1,0:T(8,128)(2,1)S(1)}) custom-call(bf16[27,8,9216]{2,1,0:T(8,128)(2,1)} %bitcast.15, bf16[8,96,128]{2,1,0:T(8,128)(2,1)} %bitcast.17), custom_call_target="tpu_custom_call" | custom-call | bytes 12000000 | tf_op jit(solution)/shard_map/spread_blocks/pallas_call | solution.py:126
  17.7 0.0 collective-permute-done.g0_ref
  17.8 0.0 collective-permute-done.1.g1_ref
  17.8 0.0 collective-permute-done.2.g2_ref
  17.8 0.0 collective-permute-done.3.g3_ref
  17.8 6.0 %make_terms.1 = bf16[32,56,128]{2,1,0:T(8,128)(2,1)S(1)} custom-call(s32[8,27]{1,0:T(8,128)} %bitcast.19, s32[8]{0:T(128)} %bitcast.22, s32[8,2,27]{2,1,0:T(2,128)} %bitcast.18, s32[16]{0:T(128)} %bitcast.23, s32[1,3,1,16]{3,2,1,0:T(1,128)} %bitcast.20, f32[27,576,128]{2,1,0:T(8,128)S(1)} %get-tuple-element.12.spread_ref, ...), custom_call_target="tpu_custom_call" | custom-call | flops 1000000000 | bytes 8000000 | tf_op jit(solution)/shard_map/make_terms/pallas_call | solution.py:261
  23.8 27.5 %all_to_all.10.recv_ref = bf16[32,56,128]{2,1,0:T(8,128)(2,1)S(1)} all-to-all(bf16[32,56,128]{2,1,0:T(8,128)(2,1)S(1)} %make_terms.1), channel_id=1, replica_groups=mesh['gx'=16,'yz'=32] {'yz'}, dimensions={0} | all-to-all | bytes 917504 | tf_op jit(solution)/shard_map/all_to_all | solution.py:368
  51.2 1.5 %sum_terms.1 = bf16[32,48,128]{2,1,0:T(8,128)(2,1)S(1)} custom-call(bf16[32,56,128]{2,1,0:T(8,128)(2,1)S(1)} %all_to_all.10.recv_ref), custom_call_target="tpu_custom_call" | custom-call | tf_op jit(solution)/shard_map/sum_terms/pallas_call | solution.py:318
  52.7 20.4 %all_to_all.11.recv_ref = bf16[32,48,128]{2,1,0:T(8,128)(2,1)S(1)} all-to-all(bf16[32,48,128]{2,1,0:T(8,128)(2,1)S(1)} %sum_terms.1), channel_id=1, replica_groups=mesh['gx'=16,'yz'=32] {'yz'}, dimensions={0} | all-to-all | bytes 786432 | tf_op jit(solution)/shard_map/all_to_all | solution.py:369
  73.1 0.9 %join_pieces.1 = f32[48,4096]{1,0:T(8,128)} custom-call(bf16[32,48,128]{2,1,0:T(8,128)(2,1)S(1)} %all_to_all.11.recv_ref), custom_call_target="tpu_custom_call" | custom-call | tf_op jit(solution)/shard_map/join_pieces/pallas_call | solution.py:340
Async XLA Ops:
  1.0 16.8 %collective-permute-start = (bf16[2,96,128]{2,1,0:T(8,128)(2,1)S(1)}, bf16[2,96,128]{2,1,0:T(8,128)(2,1)S(1)}, u32[]{:S(2)}, u32[]{:S(2)}) collective-permute-start(bf16[2,96,128]{2,1,0:T(8,128)(2,1)S(1)} %get-tuple-element.15), channel_id=1, source_target_pairs={{0,32},{64,96},{128,160},{192,224},{256,288},{320,352},{384,416},{... | collective-permute-start | bytes 147464 | tf_op jit(solution)/shard_map/ppermute | solution.py:356
  2.9 14.9 %collective-permute-start.1 = (bf16[2,96,128]{2,1,0:T(8,128)(2,1)S(1)}, bf16[2,96,128]{2,1,0:T(8,128)(2,1)S(1)}, u32[]{:S(2)}, u32[]{:S(2)}) collective-permute-start(bf16[2,96,128]{2,1,0:T(8,128)(2,1)S(1)} %get-tuple-element.16), channel_id=1, source_target_pairs={{32,64},{96,128},{160,192},{224,256},{288,320},{352,384},{416,448}... | collective-permute-start | bytes 147464 | tf_op jit(solution)/shard_map/ppermute | solution.py:356
  5.4 12.4 %collective-permute-start.2 = (bf16[2,96,128]{2,1,0:T(8,128)(2,1)S(1)}, bf16[2,96,128]{2,1,0:T(8,128)(2,1)S(1)}, u32[]{:S(2)}, u32[]{:S(2)}) collective-permute-start(bf16[2,96,128]{2,1,0:T(8,128)(2,1)S(1)} %get-tuple-element.17), channel_id=1, source_target_pairs={{0,1},{2,3},{4,5},{6,7},{8,9},{10,11},{12,13},{14,15},{16,17},{18,... | collective-permute-start | bytes 147464 | tf_op jit(solution)/shard_map/ppermute | solution.py:356
  7.3 10.5 %collective-permute-start.3 = (bf16[2,96,128]{2,1,0:T(8,128)(2,1)S(1)}, bf16[2,96,128]{2,1,0:T(8,128)(2,1)S(1)}, u32[]{:S(2)}, u32[]{:S(2)}) collective-permute-start(bf16[2,96,128]{2,1,0:T(8,128)(2,1)S(1)} %get-tuple-element.18), channel_id=1, source_target_pairs={{1,2},{3,4},{5,6},{7,8},{9,10},{11,12},{13,14},{15,16},{17,18},{19... | collective-permute-start | bytes 147464 | tf_op jit(solution)/shard_map/ppermute | solution.py:356

commit v4 on v3

--- a/solution.py
+++ b/solution.py
@@ -26,19 +26,19 @@
 VMEM_LIMIT = 20 * 1024 * 1024
 
 
-def parity(axis):
-    return lax.rem(lax.axis_index(axis), 2)
-
-
-def side_of(swap):
-    odd = parity("gx" if swap < 2 else "yz")
-    return swap // 2 * 2 + (odd if swap % 2 else 1 - odd)
-
-
-def swap_pairs(swap, size):
-    first = swap % 2
-    pairs = [(n, n + 1) for n in range(first, size - 1, 2)]
-    return pairs + [(j, i) for i, j in pairs]
+def sides():
+    odd = lax.rem(lax.axis_index("yz"), 2)
+    return 3 - odd, 2 + odd, 1, 0
+
+
+def send_rows(picked):
+    columns, slabs = lax.axis_size("yz"), lax.axis_size("gx")
+    even = [(n, n ^ 1) for n in range(columns) if n ^ 1 < columns]
+    odd = [(n, (n + 1 ^ 1) - 1) for n in range(1, columns) if n + 1 ^ 1 <= columns]
+    up = [(n, (n + 1) % slabs) for n in range(slabs)]
+    down = [(j, i) for i, j in up]
+    routes = (("yz", even), ("yz", odd), ("gx", up), ("gx", down))
+    return [lax.ppermute(rows, *route) for rows, route in zip(picked, routes)]
 
 
 def pick_kernel(glist_hbm, prolong_hbm, *refs):
@@ -51,9 +51,9 @@
         copy.start()
     for copy in copies:
         copy.wait()
-    for swap, out_ref in enumerate(out_refs):
+    for side, out_ref in zip(sides(), out_refs):
         for n in range(G):
-            out_ref[n] = prolong_ref[glist_ref[n, side_of(swap)]]
+            out_ref[n] = prolong_ref[glist_ref[n, side]]
 
 
 def pick_rows(glist, prolong):
@@ -168,8 +168,12 @@
         sum_ref[:QW] = jnp.zeros((QW, BK, LANES), jnp.float32)
     ext_ref[:NB] = own_ref[...]
     ext_ref[NB:, BK:, :] = jnp.zeros((EXT - NB, LANES - BK, LANES), jnp.bfloat16)
-    for swap, ghost_ref in enumerate((g0_ref, g1_ref, g2_ref, g3_ref)):
-        ext_ref[pl.ds(NB + side_of(swap) * G, G), :BK, :] = ghost_ref[...]
+    slab = lax.axis_index("gx")
+    here = (True, True, slab > 0, slab < lax.axis_size("gx") - 1)
+    from_side = (*sides()[:2], 0, 1)
+    for ghost_ref, side, exists in zip((g0_ref, g1_ref, g2_ref, g3_ref), from_side, here):
+        rows = ghost_ref[...]
+        ext_ref[pl.ds(NB + side * G, G), :BK, :] = jnp.where(exists, rows, jnp.zeros_like(rows))
     for copy in small:
         copy.wait()
     lane = lax.broadcasted_iota(jnp.int32, (BK // 4, LANES), 1)
@@ -350,10 +354,7 @@
 def on_device(stiffness, prolong, kcol, kcount, qslot, glist, owner, dest):
     prolong_rows = prolong[0, 0]
     picked = pick_rows(jnp.transpose(glist[0, 0]), prolong_rows)
-    ghosts = []
-    for swap, rows in enumerate(picked):
-        axis = "gx" if swap < 2 else "yz"
-        ghosts.append(lax.ppermute(rows, axis, swap_pairs(swap, lax.axis_size(axis))))
+    ghosts = send_rows(picked)
     spread, turned, own = spread_blocks(
         jnp.transpose(stiffness[0, 0], (1, 0, 2)), prolong_rows
     )

time: 74.4 us -> 71.7 us (0.964)
  starting transfers between devices: 12.9 us -> 10.3 us
    ppermute x4, starting transfers between devices: 12.9 us -> 10.3 us  [send_rows(): return [lax.ppermute(rows, *route) for rows, route in zip(picked, routes)]]
where the time goes in v4:
time: 71.7 us; the launch traced here: 71.4 us
  blocking collectives  47.8 us (67%)
  Pallas kernels  13.1 us (18%)
  starting transfers between devices  10.3 us (14%)
    all_to_all x1, blocking collectives, on_device(): lax.all_to_all(packed, 'yz', split_axis=0, concat_axis=0, tiled=True)  27.2 us
    all_to_all x1, blocking collectives, on_device(): lax.all_to_all(sum_terms(received), 'yz', split_axis=0, concat_axis=0, ti...  20.7 us
    ppermute x4, starting transfers between devices, send_rows(): return [lax.ppermute(rows, *route) for rows, route in zip(picked, routes)]  10.3 us
    pallas_call x1, Pallas kernels, make_terms(): pl.pallas_call(terms_kernel, out_shape=jax.ShapeDtypeStruct((PIECES, SEND...  5.97 us
    pallas_call x1, Pallas kernels, spread_blocks(): pl.pallas_call(spread_kernel, out_shape=[jax.ShapeDtypeStruct((KW, BK * B...  3.79 us
    pallas_call x1, Pallas kernels, sum_terms(): pl.pallas_call(sum_kernel, out_shape=jax.ShapeDtypeStruct((sources, NS, L...  1.48 us
  transfers between devices with their start and end apart: 4, of which 0 were waited for; matrix products, arithmetic and copies ran while one was open for 0% of the time, Pallas kernels for 5%

profile of v4, /device:TPU:88, one launch (start us, length us, event | category | flops | bytes accessed | tf_op | source)
XLA Modules:
  0.0 71.4 jit_solution(16857137056106491620)
XLA Ops:
  0.0 1.0 %pick_rows.1 = (bf16[2,96,128]{2,1,0:T(8,128)(2,1)S(1)}, bf16[2,96,128]{2,1,0:T(8,128)(2,1)S(1)}, bf16[2,96,128]{2,1,0:T(8,128)(2,1)S(1)}, bf16[2,96,128]{2,1,0:T(8,128)(2,1)S(1)}) custom-call(s32[2,4]{1,0:T(2,128)} %bitcast.21, bf16[8,96,128]{2,1,0:T(8,128)(2,1)} %bitcast.16), custom_call_target="tpu_custom_call" | custom-call | tf_op jit(solution)/shard_map/pick_rows/pallas_call | solution.py:61
  1.0 1.9 %collective-permute-start = (bf16[2,96,128]{2,1,0:T(8,128)(2,1)S(1)}, bf16[2,96,128]{2,1,0:T(8,128)(2,1)S(1)}, u32[]{:S(2)}, u32[]{:S(2)}) collective-permute-start(bf16[2,96,128]{2,1,0:T(8,128)(2,1)S(1)} %get-tuple-element.15), channel_id=1, source_target_pairs={{0,1},{1,0},{2,3},{3,2},{4,5},{5,4},{6,7},{7,6},{8,9},{9,8},{10,11... | collective-permute-start | bytes 147464 | tf_op jit(solution)/shard_map/ppermute | solution.py:41
  2.9 6.6 %collective-permute-start.1 = (bf16[2,96,128]{2,1,0:T(8,128)(2,1)S(1)}, bf16[2,96,128]{2,1,0:T(8,128)(2,1)S(1)}, u32[]{:S(2)}, u32[]{:S(2)}) collective-permute-start(bf16[2,96,128]{2,1,0:T(8,128)(2,1)S(1)} %get-tuple-element.16), channel_id=1, source_target_pairs={{1,2},{2,1},{3,4},{4,3},{5,6},{6,5},{7,8},{8,7},{9,10},{10,9},{11,... | collective-permute-start | bytes 147464 | tf_op jit(solution)/shard_map/ppermute | solution.py:41
  9.5 0.0 collective-permute-start.2
  9.6 1.7 %collective-permute-start.3 = (bf16[2,96,128]{2,1,0:T(8,128)(2,1)S(1)}, bf16[2,96,128]{2,1,0:T(8,128)(2,1)S(1)}, u32[]{:S(2)}, u32[]{:S(2)}) collective-permute-start(bf16[2,96,128]{2,1,0:T(8,128)(2,1)S(1)} %get-tuple-element.18), channel_id=1, source_target_pairs={{32,0},{64,32},{96,64},{128,96},{160,128},{192,160},{224,192},{256... | collective-permute-start | bytes 147464 | tf_op jit(solution)/shard_map/ppermute | solution.py:41
  11.3 3.8 %spread_blocks.1 = (f32[27,576,128]{2,1,0:T(8,128)S(1)}, bf16[8,128,96]{2,1,0:T(8,128)(2,1)S(1)}, bf16[8,128,128]{2,1,0:T(8,128)(2,1)S(1)}) custom-call(bf16[27,8,9216]{2,1,0:T(8,128)(2,1)} %bitcast.15, bf16[8,96,128]{2,1,0:T(8,128)(2,1)} %bitcast.17), custom_call_target="tpu_custom_call" | custom-call | bytes 12000000 | tf_op jit(solution)/shard_map/spread_blocks/pallas_call | solution.py:126
  15.1 0.0 collective-permute-done.g0_ref
  15.1 0.0 collective-permute-done.1.g1_ref
  15.1 0.0 collective-permute-done.2.g2_ref
  15.1 0.0 collective-permute-done.3.g3_ref
  15.1 6.0 %make_terms.1 = bf16[32,56,128]{2,1,0:T(8,128)(2,1)S(1)} custom-call(s32[8,27]{1,0:T(8,128)} %bitcast.19, s32[8]{0:T(128)} %bitcast.22, s32[8,2,27]{2,1,0:T(2,128)} %bitcast.18, s32[16]{0:T(128)} %bitcast.23, s32[1,3,1,16]{3,2,1,0:T(1,128)} %bitcast.20, f32[27,576,128]{2,1,0:T(8,128)S(1)} %get-tuple-element.12.spread_ref, ...), custom_call_target="tpu_custom_call" | custom-call | flops 1000000000 | bytes 8000000 | tf_op jit(solution)/shard_map/make_terms/pallas_call | solution.py:265
  21.1 27.2 %all_to_all.10.recv_ref = bf16[32,56,128]{2,1,0:T(8,128)(2,1)S(1)} all-to-all(bf16[32,56,128]{2,1,0:T(8,128)(2,1)S(1)} %make_terms.1), channel_id=1, replica_groups=mesh['gx'=16,'yz'=32] {'yz'}, dimensions={0} | all-to-all | bytes 917504 | tf_op jit(solution)/shard_map/all_to_all | solution.py:369
  48.3 1.5 %sum_terms.1 = bf16[32,48,128]{2,1,0:T(8,128)(2,1)S(1)} custom-call(bf16[32,56,128]{2,1,0:T(8,128)(2,1)S(1)} %all_to_all.10.recv_ref), custom_call_target="tpu_custom_call" | custom-call | tf_op jit(solution)/shard_map/sum_terms/pallas_call | solution.py:322
  49.8 20.7 %all_to_all.11.recv_ref = bf16[32,48,128]{2,1,0:T(8,128)(2,1)S(1)} all-to-all(bf16[32,48,128]{2,1,0:T(8,128)(2,1)S(1)} %sum_terms.1), channel_id=1, replica_groups=mesh['gx'=16,'yz'=32] {'yz'}, dimensions={0} | all-to-all | bytes 786432 | tf_op jit(solution)/shard_map/all_to_all | solution.py:370
  70.4 0.9 %join_pieces.1 = f32[48,4096]{1,0:T(8,128)} custom-call(bf16[32,48,128]{2,1,0:T(8,128)(2,1)S(1)} %all_to_all.11.recv_ref), custom_call_target="tpu_custom_call" | custom-call | tf_op jit(solution)/shard_map/join_pieces/pallas_call | solution.py:344
Async XLA Ops:
  1.0 14.1 %collective-permute-start = (bf16[2,96,128]{2,1,0:T(8,128)(2,1)S(1)}, bf16[2,96,128]{2,1,0:T(8,128)(2,1)S(1)}, u32[]{:S(2)}, u32[]{:S(2)}) collective-permute-start(bf16[2,96,128]{2,1,0:T(8,128)(2,1)S(1)} %get-tuple-element.15), channel_id=1, source_target_pairs={{0,1},{1,0},{2,3},{3,2},{4,5},{5,4},{6,7},{7,6},{8,9},{9,8},{10,11... | collective-permute-start | bytes 147464 | tf_op jit(solution)/shard_map/ppermute | solution.py:41
  2.9 12.2 %collective-permute-start.1 = (bf16[2,96,128]{2,1,0:T(8,128)(2,1)S(1)}, bf16[2,96,128]{2,1,0:T(8,128)(2,1)S(1)}, u32[]{:S(2)}, u32[]{:S(2)}) collective-permute-start(bf16[2,96,128]{2,1,0:T(8,128)(2,1)S(1)} %get-tuple-element.16), channel_id=1, source_target_pairs={{1,2},{2,1},{3,4},{4,3},{5,6},{6,5},{7,8},{8,7},{9,10},{10,9},{11,... | collective-permute-start | bytes 147464 | tf_op jit(solution)/shard_map/ppermute | solution.py:41
  9.5 5.6 %collective-permute-start.2 = (bf16[2,96,128]{2,1,0:T(8,128)(2,1)S(1)}, bf16[2,96,128]{2,1,0:T(8,128)(2,1)S(1)}, u32[]{:S(2)}, u32[]{:S(2)}) collective-permute-start(bf16[2,96,128]{2,1,0:T(8,128)(2,1)S(1)} %get-tuple-element.17), channel_id=1, source_target_pairs={{0,32},{32,64},{64,96},{96,128},{128,160},{160,192},{192,224},{224... | collective-permute-start | bytes 147464 | tf_op jit(solution)/shard_map/ppermute | solution.py:41
  9.6 5.6 %collective-permute-start.3 = (bf16[2,96,128]{2,1,0:T(8,128)(2,1)S(1)}, bf16[2,96,128]{2,1,0:T(8,128)(2,1)S(1)}, u32[]{:S(2)}, u32[]{:S(2)}) collective-permute-start(bf16[2,96,128]{2,1,0:T(8,128)(2,1)S(1)} %get-tuple-element.18), channel_id=1, source_target_pairs={{32,0},{64,32},{96,64},{128,96},{160,128},{192,160},{224,192},{256... | collective-permute-start | bytes 147464 | tf_op jit(solution)/shard_map/ppermute | solution.py:41

commit v5 on v4

--- a/solution.py
+++ b/solution.py
@@ -20,7 +20,7 @@
 TERMS = M * QW
 PIECES = BP * BP // LANES
 SEND_ROWS = TERMS + 8
-FLAT_PARTS = ((0, 9), (9, 18), (18, 24), (24, 27))
+FLAT_PARTS = tuple((t, t + 3) for t in range(0, KW, 3))
 UNROLL = 3
 SUM_OWNERS = 4
 VMEM_LIMIT = 20 * 1024 * 1024
@@ -111,14 +111,11 @@
     for n, (a, b) in enumerate(FLAT_PARTS):
         parts[n].wait()
 
-        def one_slot(t, carry):
+        for t in range(a, b):
             for c in range(BK * BK // LANES):
                 spread_ref[t, c * NB : (c + 1) * NB, :] = flat_ref[
                     t, :, c * LANES : (c + 1) * LANES
                 ].astype(jnp.float32)
-            return carry
-
-        lax.fori_loop(a, b, one_slot, 0)
 
 
 def spread_blocks(flat, prolong):

time: 71.7 us -> 71.6 us (level)
  no operation moved by 1% of the time
where the time goes in v5:
time: 71.6 us; the launch traced here: 71.4 us
  blocking collectives  47.8 us (67%)
  Pallas kernels  13.1 us (18%)
  starting transfers between devices  10.3 us (14%)
    all_to_all x1, blocking collectives, on_device(): lax.all_to_all(packed, 'yz', split_axis=0, concat_axis=0, tiled=True)  27.1 us
    all_to_all x1, blocking collectives, on_device(): lax.all_to_all(sum_terms(received), 'yz', split_axis=0, concat_axis=0, ti...  20.7 us
    ppermute x4, starting transfers between devices, send_rows(): return [lax.ppermute(rows, *route) for rows, route in zip(picked, routes)]  10.3 us
    pallas_call x1, Pallas kernels, make_terms(): pl.pallas_call(terms_kernel, out_shape=jax.ShapeDtypeStruct((PIECES, SEND...  5.97 us
    pallas_call x1, Pallas kernels, spread_blocks(): pl.pallas_call(spread_kernel, out_shape=[jax.ShapeDtypeStruct((KW, BK * B...  3.78 us
    pallas_call x1, Pallas kernels, sum_terms(): pl.pallas_call(sum_kernel, out_shape=jax.ShapeDtypeStruct((sources, NS, L...  1.49 us
  transfers between devices with their start and end apart: 4, of which 0 were waited for; matrix products, arithmetic and copies ran while one was open for 0% of the time, Pallas kernels for 5%

profile of v5, /device:TPU:88, one launch (start us, length us, event | category | flops | bytes accessed | tf_op | source)
XLA Modules:
  0.0 71.4 jit_solution(2815881970273497879)
XLA Ops:
  0.0 1.0 %pick_rows.1 = (bf16[2,96,128]{2,1,0:T(8,128)(2,1)S(1)}, bf16[2,96,128]{2,1,0:T(8,128)(2,1)S(1)}, bf16[2,96,128]{2,1,0:T(8,128)(2,1)S(1)}, bf16[2,96,128]{2,1,0:T(8,128)(2,1)S(1)}) custom-call(s32[2,4]{1,0:T(2,128)} %bitcast.21, bf16[8,96,128]{2,1,0:T(8,128)(2,1)} %bitcast.16), custom_call_target="tpu_custom_call" | custom-call | tf_op jit(solution)/shard_map/pick_rows/pallas_call | solution.py:61
  1.0 1.9 %collective-permute-start = (bf16[2,96,128]{2,1,0:T(8,128)(2,1)S(1)}, bf16[2,96,128]{2,1,0:T(8,128)(2,1)S(1)}, u32[]{:S(2)}, u32[]{:S(2)}) collective-permute-start(bf16[2,96,128]{2,1,0:T(8,128)(2,1)S(1)} %get-tuple-element.15), channel_id=1, source_target_pairs={{0,1},{1,0},{2,3},{3,2},{4,5},{5,4},{6,7},{7,6},{8,9},{9,8},{10,11... | collective-permute-start | bytes 147464 | tf_op jit(solution)/shard_map/ppermute | solution.py:41
  2.9 6.6 %collective-permute-start.1 = (bf16[2,96,128]{2,1,0:T(8,128)(2,1)S(1)}, bf16[2,96,128]{2,1,0:T(8,128)(2,1)S(1)}, u32[]{:S(2)}, u32[]{:S(2)}) collective-permute-start(bf16[2,96,128]{2,1,0:T(8,128)(2,1)S(1)} %get-tuple-element.16), channel_id=1, source_target_pairs={{1,2},{2,1},{3,4},{4,3},{5,6},{6,5},{7,8},{8,7},{9,10},{10,9},{11,... | collective-permute-start | bytes 147464 | tf_op jit(solution)/shard_map/ppermute | solution.py:41
  9.5 0.0 collective-permute-start.2
  9.6 1.7 %collective-permute-start.3 = (bf16[2,96,128]{2,1,0:T(8,128)(2,1)S(1)}, bf16[2,96,128]{2,1,0:T(8,128)(2,1)S(1)}, u32[]{:S(2)}, u32[]{:S(2)}) collective-permute-start(bf16[2,96,128]{2,1,0:T(8,128)(2,1)S(1)} %get-tuple-element.18), channel_id=1, source_target_pairs={{32,0},{64,32},{96,64},{128,96},{160,128},{192,160},{224,192},{256... | collective-permute-start | bytes 147464 | tf_op jit(solution)/shard_map/ppermute | solution.py:41
  11.3 3.8 %spread_blocks.1 = (f32[27,576,128]{2,1,0:T(8,128)S(1)}, bf16[8,128,96]{2,1,0:T(8,128)(2,1)S(1)}, bf16[8,128,128]{2,1,0:T(8,128)(2,1)S(1)}) custom-call(bf16[27,8,9216]{2,1,0:T(8,128)(2,1)} %bitcast.15, bf16[8,96,128]{2,1,0:T(8,128)(2,1)} %bitcast.17), custom_call_target="tpu_custom_call" | custom-call | bytes 12000000 | tf_op jit(solution)/shard_map/spread_blocks/pallas_call | solution.py:123
  15.1 0.0 collective-permute-done.g0_ref
  15.1 0.0 collective-permute-done.1.g1_ref
  15.1 0.0 collective-permute-done.2.g2_ref
  15.1 0.0 collective-permute-done.3.g3_ref
  15.1 6.0 %make_terms.1 = bf16[32,56,128]{2,1,0:T(8,128)(2,1)S(1)} custom-call(s32[8,27]{1,0:T(8,128)} %bitcast.19, s32[8]{0:T(128)} %bitcast.22, s32[8,2,27]{2,1,0:T(2,128)} %bitcast.18, s32[16]{0:T(128)} %bitcast.23, s32[1,3,1,16]{3,2,1,0:T(1,128)} %bitcast.20, f32[27,576,128]{2,1,0:T(8,128)S(1)} %get-tuple-element.12.spread_ref, ...), custom_call_target="tpu_custom_call" | custom-call | flops 1000000000 | bytes 8000000 | tf_op jit(solution)/shard_map/make_terms/pallas_call | solution.py:262
  21.1 27.1 %all_to_all.10.recv_ref = bf16[32,56,128]{2,1,0:T(8,128)(2,1)S(1)} all-to-all(bf16[32,56,128]{2,1,0:T(8,128)(2,1)S(1)} %make_terms.1), channel_id=1, replica_groups=mesh['gx'=16,'yz'=32] {'yz'}, dimensions={0} | all-to-all | bytes 917504 | tf_op jit(solution)/shard_map/all_to_all | solution.py:366
  48.2 1.5 %sum_terms.1 = bf16[32,48,128]{2,1,0:T(8,128)(2,1)S(1)} custom-call(bf16[32,56,128]{2,1,0:T(8,128)(2,1)S(1)} %all_to_all.10.recv_ref), custom_call_target="tpu_custom_call" | custom-call | tf_op jit(solution)/shard_map/sum_terms/pallas_call | solution.py:319
  49.7 20.7 %all_to_all.11.recv_ref = bf16[32,48,128]{2,1,0:T(8,128)(2,1)S(1)} all-to-all(bf16[32,48,128]{2,1,0:T(8,128)(2,1)S(1)} %sum_terms.1), channel_id=1, replica_groups=mesh['gx'=16,'yz'=32] {'yz'}, dimensions={0} | all-to-all | bytes 786432 | tf_op jit(solution)/shard_map/all_to_all | solution.py:367
  70.4 0.9 %join_pieces.1 = f32[48,4096]{1,0:T(8,128)} custom-call(bf16[32,48,128]{2,1,0:T(8,128)(2,1)S(1)} %all_to_all.11.recv_ref), custom_call_target="tpu_custom_call" | custom-call | tf_op jit(solution)/shard_map/join_pieces/pallas_call | solution.py:341
Async XLA Ops:
  1.0 14.1 %collective-permute-start = (bf16[2,96,128]{2,1,0:T(8,128)(2,1)S(1)}, bf16[2,96,128]{2,1,0:T(8,128)(2,1)S(1)}, u32[]{:S(2)}, u32[]{:S(2)}) collective-permute-start(bf16[2,96,128]{2,1,0:T(8,128)(2,1)S(1)} %get-tuple-element.15), channel_id=1, source_target_pairs={{0,1},{1,0},{2,3},{3,2},{4,5},{5,4},{6,7},{7,6},{8,9},{9,8},{10,11... | collective-permute-start | bytes 147464 | tf_op jit(solution)/shard_map/ppermute | solution.py:41
  2.9 12.2 %collective-permute-start.1 = (bf16[2,96,128]{2,1,0:T(8,128)(2,1)S(1)}, bf16[2,96,128]{2,1,0:T(8,128)(2,1)S(1)}, u32[]{:S(2)}, u32[]{:S(2)}) collective-permute-start(bf16[2,96,128]{2,1,0:T(8,128)(2,1)S(1)} %get-tuple-element.16), channel_id=1, source_target_pairs={{1,2},{2,1},{3,4},{4,3},{5,6},{6,5},{7,8},{8,7},{9,10},{10,9},{11,... | collective-permute-start | bytes 147464 | tf_op jit(solution)/shard_map/ppermute | solution.py:41
  9.5 5.6 %collective-permute-start.2 = (bf16[2,96,128]{2,1,0:T(8,128)(2,1)S(1)}, bf16[2,96,128]{2,1,0:T(8,128)(2,1)S(1)}, u32[]{:S(2)}, u32[]{:S(2)}) collective-permute-start(bf16[2,96,128]{2,1,0:T(8,128)(2,1)S(1)} %get-tuple-element.17), channel_id=1, source_target_pairs={{0,32},{32,64},{64,96},{96,128},{128,160},{160,192},{192,224},{224... | collective-permute-start | bytes 147464 | tf_op jit(solution)/shard_map/ppermute | solution.py:41
  9.6 5.6 %collective-permute-start.3 = (bf16[2,96,128]{2,1,0:T(8,128)(2,1)S(1)}, bf16[2,96,128]{2,1,0:T(8,128)(2,1)S(1)}, u32[]{:S(2)}, u32[]{:S(2)}) collective-permute-start(bf16[2,96,128]{2,1,0:T(8,128)(2,1)S(1)} %get-tuple-element.18), channel_id=1, source_target_pairs={{32,0},{64,32},{96,64},{128,96},{160,128},{192,160},{224,192},{256... | collective-permute-start | bytes 147464 | tf_op jit(solution)/shard_map/ppermute | solution.py:41
